TPU v7x, 512 devices: a whole 4x8x8 slice. The times are simulated.
512 devices in a mesh: blk: 128 (over y_hi, z, x), mp: 4 (over y_lo, core).
Axes of the slice: x: 4, y: 8 (y_hi: 4, y_lo: 2; y = y_hi * 2 + y_lo), z: 8, core: 2. Of those that a mesh axis runs over, the one named last changes fastest.
Arguments:
- queries: bfloat16 [1024, 32, 128], P(('blk', 'mp')), may hold values from -32 to 32
- passages: bfloat16 [1024, 180, 128], P(('blk', 'mp')), may hold values from -32 to 32
- lengths: int32 [1024], P(('blk', 'mp')), may hold values from 45 to 180
- pos_index: int32 [128, 8], P('blk'), may hold values from 0 to 7, each once within a row
Outputs:
- query_loss: float32 [1024], P(('blk', 'mp'))
- query_grads: float32 [1024, 32, 128], P(('blk', 'mp'))
- passage_grads: float32 [1024, 180, 128], P(('blk', 'mp'))
Inputs may be any that keep to these rules, and one draw needn't show every extreme that they name: Each row of pos_index holds every number of 0 to 7 once.
All inputs are finite; a program needn't handle non-finite values.
Results may differ from a plain program's by a relative error of at most 0.0035.
Values may be sent and summed in bfloat16 or wider, within the bound.
A program may use at most 64 MiB of HBM per device.

v0:
```python
import jax
import jax.numpy as jnp
from jax import lax
from jax.sharding import PartitionSpec as P

WINDOW = 4


NEG = -1e30


def passed_along(shard, axis, by):
    devices = lax.axis_size(axis)
    return lax.ppermute(shard, axis, [(i, (i + by) % devices) for i in range(devices)])


def merged(shard, axis, combine):
    everything = jax.tree.map(lambda part: lax.all_gather(part, axis), shard)
    first = jax.tree.map(lambda part: part[0], everything)

    def step(k, so_far):
        return combine(so_far, jax.tree.map(lambda part: part[k], everything))

    return lax.fori_loop(1, lax.axis_size(axis), step, first)


def combine_totals(earlier, later):
    maximum = jnp.maximum(earlier[0], later[0])
    return (
        maximum,
        earlier[1] * jnp.exp(earlier[0] - maximum) + later[1] * jnp.exp(later[0] - maximum),
    )


def tile_terms(query_group, pass_rows, usable, log_length, inv_root):
    group_size, query_tok, feat_dim = query_group.shape
    per_dev, pass_tok = usable.shape
    logits = (
        lax.dot_general(
            query_group.reshape(group_size * query_tok, feat_dim),
            pass_rows,
            (((1,), (1,)), ((), ())),
            preferred_element_type=jnp.float32,
        )
        * inv_root
    )
    logits = logits.reshape(group_size, query_tok, per_dev, pass_tok)
    masked = jnp.where(usable[None, None], logits, NEG)
    maximum = jnp.max(masked, axis=3)
    exp_terms = jnp.where(usable[None, None], jnp.exp(masked - maximum[..., None]), 0.0)
    sums_exp = jnp.sum(exp_terms, axis=3)
    scores = jnp.sum(maximum + jnp.log(sums_exp) - log_length[None, None, :], axis=1)
    return (scores, exp_terms, sums_exp)


def on_device(queries, passages, lengths, pos_index):
    per_dev, query_tok, feat_dim = queries.shape
    pass_tok = passages.shape[1]
    inv_root = feat_dim ** (-0.5)
    mp_index = lax.axis_index("mp")
    pass_rows = passages.reshape(per_dev * pass_tok, feat_dim)
    usable = jnp.arange(pass_tok)[None, :] < lengths[:, None]
    log_length = jnp.log(lengths.astype(jnp.float32))
    held_block = lax.all_gather(queries, "mp", axis=0, tiled=True)
    block_pairs = held_block.shape[0]
    group_size = min(16, block_pairs)
    group_count = block_pairs // group_size
    local_col = pos_index[0] - mp_index * per_dev
    positive = (jnp.arange(per_dev)[None, :] == local_col[:, None]).astype(jnp.float32)
    travel = held_block
    totals = None
    pos_local = None
    met_blocks = []
    for cycle_step in range(WINDOW):
        if cycle_step > 0:
            travel = passed_along(travel, "blk", 1)
            totals = passed_along(totals, "blk", 1)
        met_blocks.append(travel)

        def group_scores(query_group):
            return tile_terms(query_group, pass_rows, usable, log_length, inv_root)[0]

        grouped = travel.reshape(group_count, group_size, query_tok, feat_dim)
        scores = lax.map(group_scores, grouped).reshape(block_pairs, per_dev)
        if cycle_step == 0:
            pos_local = jnp.sum(scores * positive, axis=1)
        maximum = jnp.max(scores, axis=1)
        partial_value = (maximum, jnp.sum(jnp.exp(scores - maximum[:, None]), axis=1))
        partial_value = merged(partial_value, "mp", combine_totals)
        totals = partial_value if cycle_step == 0 else combine_totals(totals, partial_value)
    row_lse = totals[0] + jnp.log(totals[1])
    pos_score = lax.psum_scatter(pos_local, "mp", scatter_dimension=0, tiled=True)
    pass_total = jnp.zeros((per_dev * pass_tok, feat_dim), jnp.float32)
    lse_mine = passed_along(row_lse, "blk", 1 - WINDOW)
    travel = held_block
    carried = (lse_mine, jnp.zeros((block_pairs, query_tok, feat_dim), jnp.float32))
    for cycle_step in range(WINDOW):
        if cycle_step > 0:
            travel = passed_along(travel, "blk", 1)
            carried = passed_along((carried[0], carried[1]), "blk", 1)
        hit_scale = 1.0 if cycle_step == 0 else 0.0

        def group_step(pass_grad, operands):
            query_group, lse_group, hit_group = operands
            scores, exp_terms, sums_exp = tile_terms(
                query_group, pass_rows, usable, log_length, inv_root
            )
            coef = jnp.exp(scores - lse_group[:, None]) - hit_group
            weights = exp_terms / sums_exp[..., None]
            dlogit = (coef[:, None, :, None] * weights).astype(jnp.bfloat16)
            dlogit = dlogit.reshape(group_size * query_tok, per_dev * pass_tok)
            query_grad = jnp.dot(dlogit, pass_rows, preferred_element_type=jnp.float32) * inv_root
            rows_flat = query_group.reshape(group_size * query_tok, feat_dim)
            pass_grad = (
                pass_grad
                + lax.dot_general(
                    dlogit, rows_flat, (((0,), (0,)), ((), ())), preferred_element_type=jnp.float32
                )
                * inv_root
            )
            return (pass_grad, query_grad.reshape(group_size, query_tok, feat_dim))

        operands = (
            travel.reshape(group_count, group_size, query_tok, feat_dim),
            carried[0].reshape(group_count, group_size),
            (positive * hit_scale).reshape(group_count, group_size, per_dev),
        )
        start_grad = jnp.zeros((per_dev * pass_tok, feat_dim), jnp.float32)
        pass_grad, query_grad = lax.scan(group_step, start_grad, operands)
        query_grad, pass_grad = (query_grad.reshape(block_pairs, query_tok, feat_dim), pass_grad)
        carried = (carried[0], carried[1] + query_grad)
        pass_total = pass_total + pass_grad
    grad_home = passed_along(carried[1], "blk", 1 - WINDOW)
    own_lse = lax.dynamic_slice_in_dim(lse_mine, mp_index * per_dev, per_dev)
    query_loss = own_lse - pos_score
    query_grads = lax.psum_scatter(grad_home, "mp", scatter_dimension=0, tiled=True)
    return (query_loss, query_grads, pass_total.reshape(per_dev, pass_tok, feat_dim))


def solution(mesh):
    placed = (
        P(("blk", "mp"), None, None),
        P(("blk", "mp"), None, None),
        P(("blk", "mp")),
        P("blk", None),
    )
    return jax.shard_map(
        on_device,
        mesh=mesh,
        in_specs=placed,
        out_specs=(P(("blk", "mp")), P(("blk", "mp"), None, None), P(("blk", "mp"), None, None)),
        check_vma=False,
    )
```

profile of v0, /device:TPU:1, one launch (start us, length us, event | category | flops | bytes accessed | tf_op | source)
XLA Modules:
  0.0 248.3 jit_solution(14480711098557202323)
XLA Ops:
  7.2 12.2 %all_gather.51 = bf16[8,32,128]{2,1,0:T(8,128)(2,1)S(1)} all-gather(bf16[2,32,128]{2,1,0:T(8,128)(2,1)} %param.12), channel_id=1, replica_groups=mesh['blk'=128,'mp'=4] {'mp'}, dimensions={0}, use_global_device_ids=true | all-gather | bytes 81920 | tf_op jit(solution)/shard_map/all_gather | solution.py:64
  26.5 7.3 %collective-permute-done.1 = bf16[8,32,128]{2,1,0:T(8,128)(2,1)S(1)} collective-permute-done((bf16[8,32,128]{2,1,0:T(8,128)(2,1)S(1)}, bf16[8,32,128]{2,1,0:T(8,128)(2,1)S(1)}, u32[]{:S(2)}, u32[]{:S(2)}) %collective-permute-start.1) | collective-permute-done | bytes 65568 | tf_op jit(solution)/shard_map/ppermute | solution.py:14
  33.8 1.9 collective-permute-start.3
  36.6 10.7 %collective-permute-done.3 = bf16[8,32,128]{2,1,0:T(8,128)(2,1)} collective-permute-done((bf16[8,32,128]{2,1,0:T(8,128)(2,1)S(1)}, bf16[8,32,128]{2,1,0:T(8,128)(2,1)}, u32[]{:S(2)}, u32[]{:S(2)}) %collective-permute-start.3) | collective-permute-done | bytes 65568 | tf_op jit(solution)/shard_map/ppermute | solution.py:14
  49.0 1.9 collective-permute-start.5
  65.0 3.3 %select_reduce_fusion.1 = (f32[8,32,2]{2,1,0:T(8,128)S(1)}, f32[8,32,2]{2,1,0:T(8,128)S(1)}, f32[8,32,2]{2,1,0:T(8,128)S(1)}, f32[8,32,2]{2,1,0:T(8,128)S(1)}) fusion(pred[2,180]{1,0:T(4,128)(4,1)S(1)} %iota_compare_fusion.1, f32[8,32,2,180]{3,2,1,0:T(2,128)S(1)} %reshape.339, f32[8,32,2]{2,1,0:T(8,128)S(1)} %get-tuple-element.738, ...), kind=kLoop, calls=%fused_computation.37 | loop fusion | flops 1103872 | bytes 1487208 | tf_op jit(solution)/shard_map/while/body/eval_jaxpr/reduce_sum | solution.py:51
  72.9 6.8 %all-reduce.9 = (f32[8]{0:T(128)S(1)}, f32[32]{0:T(128)S(1)}, f32[32]{0:T(128)S(1)}, f32[32]{0:T(128)S(1)}, f32[32]{0:T(128)S(1)}, /*index=5*/f32[32]{0:T(128)S(...) all-reduce(f32[8]{0:T(128)S(1)} %get-tuple-element.733, ...), channel_id=10, replica_groups=mesh['blk'=128,'mp'=4] {'mp'}, use_global_device_ids=true, to_apply=%region_29.30.clone | all-reduce | flops 264 | bytes 2112
  80.8 1.9 collective-permute-start.6
  82.7 2.1 collective-permute-start
  95.0 1.9 collective-permute-start.7
  96.9 1.9 collective-permute-start.2
  98.9 6.8 %collective-permute-done.7 = f32[8]{0:T(128)S(1)} collective-permute-done((f32[8]{0:T(128)S(1)}, f32[8]{0:T(128)S(1)}, u32[]{:S(2)}, u32[]{:S(2)}) %collective-permute-start.7) | collective-permute-done | bytes 64 | tf_op jit(solution)/shard_map/ppermute | solution.py:14
  105.6 1.9 collective-permute-done.2
  107.6 1.9 collective-permute-start.8
  109.5 1.9 collective-permute-start.4
  111.4 6.8 %collective-permute-done.8 = f32[8]{0:T(128)S(1)} collective-permute-done((f32[8]{0:T(128)S(1)}, f32[8]{0:T(128)S(1)}, u32[]{:S(2)}, u32[]{:S(2)}) %collective-permute-start.8) | collective-permute-done | bytes 64 | tf_op jit(solution)/shard_map/ppermute | solution.py:14
  118.2 1.9 collective-permute-done.4
  120.1 1.9 collective-permute-start.9
  122.1 3.6 %collective-permute-done.9 = f32[8]{0:T(128)S(1)} collective-permute-done((f32[8]{0:T(128)S(1)}, f32[8]{0:T(128)S(1)}, u32[]{:S(2)}, u32[]{:S(2)}) %collective-permute-start.9) | collective-permute-done | bytes 64 | tf_op jit(solution)/shard_map/ppermute | solution.py:14
  129.8 8.1 %collective-permute-done.11 = f32[8]{0:T(128)S(1)} collective-permute-done((f32[8]{0:T(128)S(1)}, f32[8]{0:T(128)S(1)}, u32[]{:S(2)}, u32[]{:S(2)}) %collective-permute-start.11) | collective-permute-done | bytes 64 | tf_op jit(solution)/shard_map/ppermute | solution.py:14
  141.4 8.7 %collective-permute-done.13 = f32[8]{0:T(128)S(1)} collective-permute-done((f32[8]{0:T(128)S(1)}, f32[8]{0:T(128)S(1)}, u32[]{:S(2)}, u32[]{:S(2)}) %collective-permute-start.13) | collective-permute-done | bytes 64 | tf_op jit(solution)/shard_map/ppermute | solution.py:14
  153.7 8.7 %collective-permute-done.15 = f32[8]{0:T(128)S(1)} collective-permute-done((f32[8]{0:T(128)S(1)}, f32[8]{0:T(128)S(1)}, u32[]{:S(2)}, u32[]{:S(2)}) %collective-permute-start.15) | collective-permute-done | bytes 64 | tf_op jit(solution)/shard_map/ppermute | solution.py:14
  164.3 2.6 %multiply_convert_fusion = (bf16[256,360]{0,1:T(8,128)(2,1)S(1)}, bf16[256,360]{0,1:T(8,128)(2,1)S(1)}, bf16[256,360]{0,1:T(8,128)(2,1)S(1)}, bf16[256,360]{0,1:T(8,128)(2,1)S(1)}) fusion(f32[256,360]{0,1:T(8,128)} %copy.42, f32[256,360]{0,1:T(8,128)} %copy.41, f32[256,360]{0,1:T(8,128)} %copy.40, f32[256,360]{0,1:T(8,128)S(1)} %copy-done.1, ...), kind=kLoop, calls=%fused_computation.48 | loop fusion | flops 2211840 | bytes 6635880 | tf_op jit(solution)/shard_map/while/body/eval_jaxpr/convert_element_type | solution.py:110
  167.3 1.9 collective-permute-start.10
  169.5 10.2 %collective-permute-done.10 = f32[8,32,128]{2,1,0:T(8,128)S(1)} collective-permute-done((f32[8,32,128]{2,1,0:T(8,128)S(1)}, f32[8,32,128]{2,1,0:T(8,128)S(1)}, u32[]{:S(2)}, u32[]{:S(2)}) %collective-permute-start.10) | collective-permute-done | bytes 131104 | tf_op jit(solution)/shard_map/ppermute | solution.py:14
  179.8 1.9 collective-permute-start.12
  181.9 9.9 %collective-permute-done.12 = f32[8,32,128]{2,1,0:T(8,128)S(1)} collective-permute-done((f32[8,32,128]{2,1,0:T(8,128)S(1)}, f32[8,32,128]{2,1,0:T(8,128)S(1)}, u32[]{:S(2)}, u32[]{:S(2)}) %collective-permute-start.12) | collective-permute-done | bytes 131104 | tf_op jit(solution)/shard_map/ppermute | solution.py:14
  191.9 1.9 collective-permute-start.14
  194.1 10.0 %collective-permute-done.14 = f32[8,32,128]{2,1,0:T(8,128)S(1)} collective-permute-done((f32[8,32,128]{2,1,0:T(8,128)S(1)}, f32[8,32,128]{2,1,0:T(8,128)S(1)}, u32[]{:S(2)}, u32[]{:S(2)}) %collective-permute-start.14) | collective-permute-done | bytes 131104 | tf_op jit(solution)/shard_map/ppermute | solution.py:14
  204.0 1.9 collective-permute-start.16
  206.2 4.8 %collective-permute-done.16 = f32[8,32,128]{2,1,0:T(8,128)S(1)} collective-permute-done((f32[8,32,128]{2,1,0:T(8,128)S(1)}, f32[8,32,128]{2,1,0:T(8,128)S(1)}, u32[]{:S(2)}, u32[]{:S(2)}) %collective-permute-start.16) | collective-permute-done | bytes 131104 | tf_op jit(solution)/shard_map/ppermute | solution.py:14
  214.5 27.0 %reduce-scatter.2.cloned.1.call-done = f32[2,32,128]{2,1,0:T(8,128)} async-done(((f32[8,32,128]{2,1,0:T(8,128)}), f32[2,32,128]{2,1,0:T(8,128)}) %reduce-scatter.2.cloned.1.call-update) | async-done | bytes 32784 | tf_op jit(solution)/shard_map/reduce_scatter | solution.py:136
  (180 shorter events, 56.4 us)
Async XLA Ops:
  7.2 15.6 %copy-start.17 = (bf16[2,180,128]{2,0,1:T(2,128)(2,1)S(1)}, bf16[2,180,128]{2,0,1:T(2,128)(2,1)}, u32[]{:S(2)}) copy-start(bf16[2,180,128]{2,0,1:T(2,128)(2,1)} %param.13) | copy-start | bytes 276484
  7.2 234.3 %reduce-scatter.2.cloned.1.call-start = ((), (), s32[]{:S(2)}) async-start(), calls=%async_computation.1 | async-start | bytes 163840 | tf_op jit(solution)/shard_map/reduce_scatter | solution.py:136
  19.4 14.4 %collective-permute-start.1 = (bf16[8,32,128]{2,1,0:T(8,128)(2,1)S(1)}, bf16[8,32,128]{2,1,0:T(8,128)(2,1)S(1)}, u32[]{:S(2)}, u32[]{:S(2)}) collective-permute-start(bf16[8,32,128]{2,1,0:T(8,128)(2,1)S(1)} %all_gather.51), channel_id=1, source_target_pairs={{0,4},{4,8},{8,12},{12,16},{16,20},{20,24},{24,28},{28,32},{32,36}... | collective-permute-start | bytes 196616 | tf_op jit(solution)/shard_map/ppermute | solution.py:14
  33.8 2.2 copy-start.14
  33.8 13.5 %collective-permute-start.3 = (bf16[8,32,128]{2,1,0:T(8,128)(2,1)S(1)}, bf16[8,32,128]{2,1,0:T(8,128)(2,1)}, u32[]{:S(2)}, u32[]{:S(2)}) collective-permute-start(bf16[8,32,128]{2,1,0:T(8,128)(2,1)S(1)} %collective-permute-done.1), channel_id=1, source_target_pairs={{0,4},{4,8},{8,12},{12,16},{16,20},{20,24},{24,28},{28,32},{32,36}... | collective-permute-start | bytes 196616 | tf_op jit(solution)/shard_map/ppermute | solution.py:14
  49.0 11.8 %collective-permute-start.5 = (bf16[8,32,128]{2,1,0:T(8,128)(2,1)}, bf16[8,32,128]{2,1,0:T(8,128)(2,1)}, u32[]{:S(2)}, u32[]{:S(2)}) collective-permute-start(bf16[8,32,128]{2,1,0:T(8,128)(2,1)} %collective-permute-done.3), channel_id=1, source_target_pairs={{0,4},{4,8},{8,12},{12,16},{16,20},{20,24},{24,28},{28,32},{32,36}... | collective-permute-start | bytes 196616 | tf_op jit(solution)/shard_map/ppermute | solution.py:14
  68.3 1.7 copy-start.4
  68.3 1.7 copy-start.6
  68.3 1.7 copy-start.10
  68.3 1.7 copy-start.12
  68.3 1.7 copy-start.3
  80.1 4.7 %copy-start.13 = (f32[8,32,2]{2,1,0:T(8,128)S(1)}, f32[8,32,2]{2,1,0:T(8,128)}, u32[]{:S(2)}) copy-start(f32[8,32,2]{2,1,0:T(8,128)} %copy-done.12) | copy-start | bytes 6148
  80.8 14.2 %collective-permute-start.6 = (f32[8]{0:T(128)S(1)}, f32[8]{0:T(128)S(1)}, u32[]{:S(2)}, u32[]{:S(2)}) collective-permute-start(f32[8]{0:T(128)S(1)} %get-tuple-element.719), channel_id=1, source_target_pairs={{0,4},{4,8},{8,12},{12,16},{16,20},{20,24},{24,28},{28,32},{32,36}... | collective-permute-start | bytes 104 | tf_op jit(solution)/shard_map/ppermute | solution.py:14
  82.7 12.3 %collective-permute-start = (f32[8]{0:T(128)S(1)}, f32[8]{0:T(128)S(1)}, u32[]{:S(2)}, u32[]{:S(2)}) collective-permute-start(f32[8]{0:T(128)S(1)} %get-tuple-element.715), channel_id=1, source_target_pairs={{0,4},{4,8},{8,12},{12,16},{16,20},{20,24},{24,28},{28,32},{32,36}... | collective-permute-start | bytes 104 | tf_op jit(solution)/shard_map/ppermute | solution.py:14
  90.7 0.9 copy-start.5
  92.4 0.9 copy-start.11
  95.0 10.6 %collective-permute-start.7 = (f32[8]{0:T(128)S(1)}, f32[8]{0:T(128)S(1)}, u32[]{:S(2)}, u32[]{:S(2)}) collective-permute-start(f32[8]{0:T(128)S(1)} %get-tuple-element.805), channel_id=1, source_target_pairs={{0,4},{4,8},{8,12},{12,16},{16,20},{20,24},{24,28},{28,32},{32,36}... | collective-permute-start | bytes 104 | tf_op jit(solution)/shard_map/ppermute | solution.py:14
  96.9 10.6 %collective-permute-start.2 = (f32[8]{0:T(128)S(1)}, f32[8]{0:T(128)S(1)}, u32[]{:S(2)}, u32[]{:S(2)}) collective-permute-start(f32[8]{0:T(128)S(1)} %get-tuple-element.806), channel_id=1, source_target_pairs={{0,4},{4,8},{8,12},{12,16},{16,20},{20,24},{24,28},{28,32},{32,36}... | collective-permute-start | bytes 104 | tf_op jit(solution)/shard_map/ppermute | solution.py:14
  107.6 10.6 %collective-permute-start.8 = (f32[8]{0:T(128)S(1)}, f32[8]{0:T(128)S(1)}, u32[]{:S(2)}, u32[]{:S(2)}) collective-permute-start(f32[8]{0:T(128)S(1)} %get-tuple-element.803), channel_id=1, source_target_pairs={{0,4},{4,8},{8,12},{12,16},{16,20},{20,24},{24,28},{28,32},{32,36}... | collective-permute-start | bytes 104 | tf_op jit(solution)/shard_map/ppermute | solution.py:14
  109.5 10.6 %collective-permute-start.4 = (f32[8]{0:T(128)S(1)}, f32[8]{0:T(128)S(1)}, u32[]{:S(2)}, u32[]{:S(2)}) collective-permute-start(f32[8]{0:T(128)S(1)} %get-tuple-element.804), channel_id=1, source_target_pairs={{0,4},{4,8},{8,12},{12,16},{16,20},{20,24},{24,28},{28,32},{32,36}... | collective-permute-start | bytes 104 | tf_op jit(solution)/shard_map/ppermute | solution.py:14
  120.1 5.5 %collective-permute-start.9 = (f32[8]{0:T(128)S(1)}, f32[8]{0:T(128)S(1)}, u32[]{:S(2)}, u32[]{:S(2)}) collective-permute-start(f32[8]{0:T(128)S(1)} %log_add_fusion), channel_id=1, source_target_pairs={{0,500},{4,504},{8,508},{12,0},{16,4},{20,8},{24,12},{28,16},{32,2... | collective-permute-start | bytes 104 | tf_op jit(solution)/shard_map/ppermute | solution.py:14
  127.3 10.6 %collective-permute-start.11 = (f32[8]{0:T(128)S(1)}, f32[8]{0:T(128)S(1)}, u32[]{:S(2)}, u32[]{:S(2)}) collective-permute-start(f32[8]{0:T(128)S(1)} %collective-permute-done.9), channel_id=1, source_target_pairs={{0,4},{4,8},{8,12},{12,16},{16,20},{20,24},{24,28},{28,32},{32,36}... | collective-permute-start | bytes 104 | tf_op jit(solution)/shard_map/ppermute | solution.py:14
  139.5 10.6 %collective-permute-start.13 = (f32[8]{0:T(128)S(1)}, f32[8]{0:T(128)S(1)}, u32[]{:S(2)}, u32[]{:S(2)}) collective-permute-start(f32[8]{0:T(128)S(1)} %collective-permute-done.11), channel_id=1, source_target_pairs={{0,4},{4,8},{8,12},{12,16},{16,20},{20,24},{24,28},{28,32},{32,36}... | collective-permute-start | bytes 104 | tf_op jit(solution)/shard_map/ppermute | solution.py:14
  151.8 10.6 %collective-permute-start.15 = (f32[8]{0:T(128)S(1)}, f32[8]{0:T(128)S(1)}, u32[]{:S(2)}, u32[]{:S(2)}) collective-permute-start(f32[8]{0:T(128)S(1)} %collective-permute-done.13), channel_id=1, source_target_pairs={{0,4},{4,8},{8,12},{12,16},{16,20},{20,24},{24,28},{28,32},{32,36}... | collective-permute-start | bytes 104 | tf_op jit(solution)/shard_map/ppermute | solution.py:14
  162.7 1.4 copy-start.9
  163.1 1.0 copy-start.1
  163.1 1.2 copy-start.8
  167.3 12.4 %collective-permute-start.10 = (f32[8,32,128]{2,1,0:T(8,128)S(1)}, f32[8,32,128]{2,1,0:T(8,128)S(1)}, u32[]{:S(2)}, u32[]{:S(2)}) collective-permute-start(f32[8,32,128]{2,1,0:T(8,128)S(1)} %bitcast.107), channel_id=1, source_target_pairs={{0,4},{4,8},{8,12},{12,16},{16,20},{20,24},{24,28},{28,32},{32,36}... | collective-permute-start | bytes 393224 | tf_op jit(solution)/shard_map/ppermute | solution.py:14
  179.8 12.1 %collective-permute-start.12 = (f32[8,32,128]{2,1,0:T(8,128)S(1)}, f32[8,32,128]{2,1,0:T(8,128)S(1)}, u32[]{:S(2)}, u32[]{:S(2)}) collective-permute-start(f32[8,32,128]{2,1,0:T(8,128)S(1)} %add.270), channel_id=1, source_target_pairs={{0,4},{4,8},{8,12},{12,16},{16,20},{20,24},{24,28},{28,32},{32,36}... | collective-permute-start | bytes 393224 | tf_op jit(solution)/shard_map/ppermute | solution.py:14
  191.9 12.1 %collective-permute-start.14 = (f32[8,32,128]{2,1,0:T(8,128)S(1)}, f32[8,32,128]{2,1,0:T(8,128)S(1)}, u32[]{:S(2)}, u32[]{:S(2)}) collective-permute-start(f32[8,32,128]{2,1,0:T(8,128)S(1)} %add.271), channel_id=1, source_target_pairs={{0,4},{4,8},{8,12},{12,16},{16,20},{20,24},{24,28},{28,32},{32,36}... | collective-permute-start | bytes 393224 | tf_op jit(solution)/shard_map/ppermute | solution.py:14
  204.0 2.0 copy-start.15
  204.0 6.9 %collective-permute-start.16 = (f32[8,32,128]{2,1,0:T(8,128)S(1)}, f32[8,32,128]{2,1,0:T(8,128)S(1)}, u32[]{:S(2)}, u32[]{:S(2)}) collective-permute-start(f32[8,32,128]{2,1,0:T(8,128)S(1)} %add.272), channel_id=1, source_target_pairs={{0,500},{4,504},{8,508},{12,0},{16,4},{20,8},{24,12},{28,16},{32,2... | collective-permute-start | bytes 393224 | tf_op jit(solution)/shard_map/ppermute | solution.py:14
  (7 other events, 5.0 us)
Sparse Core Ops, SparseCore 0:
  211.7 29.7 reduce-scatter.1
where the time goes:
time: 249 us; the launch traced here: 248 us
  waiting for transfers between devices  128 us (51%)
  local copies, waits for them, and re-layouts  35.6 us (14%)
  starting transfers between devices  32.8 us (13%)
  blocking collectives  19 us (8%)
  between operations  16.1 us (6%)
  other arithmetic  10.6 us (4%)
  matrix products  6.2 us (2%)
    ppermute x17, waiting for transfers between devices, passed_along(): lax.ppermute(shard, axis, [(i, (i + by) % devices) for i in range(devices)])  101 us
    ppermute x17, starting transfers between devices, passed_along(): lax.ppermute(shard, axis, [(i, (i + by) % devices) for i in range(devices)])  32.8 us
    reduce_scatter x1, waiting for transfers between devices, on_device(): lax.psum_scatter(grad_home, 'mp', scatter_dimension=0, tiled=True)  27 us
    all_gather x1, blocking collectives, on_device(): held_block = lax.all_gather(queries, 'mp', axis=0, tiled=True)  12.2 us
    sub x12, local copies, waits for them, and re-layouts, tile_terms(): masked - maximum[..., None]  10.1 us
    unnamed x61, local copies, waits for them, and re-layouts  7.42 us
    unnamed x1, blocking collectives  6.79 us
    div x12, local copies, waits for them, and re-layouts, group_step(): weights = exp_terms / sums_exp[..., None]  6.69 us
  transfers between devices with their start and end apart: 18, of which 16 were waited for; matrix products, arithmetic and copies ran while one was open for 10% of the time, Pallas kernels for 0%

commit v1 on v0

v1 whole, which is shorter than its diff:
```python
import functools
import math

import jax
import jax.numpy as jnp
from jax import lax
from jax.experimental import pallas as pl
from jax.experimental.pallas import tpu as pltpu
from jax.sharding import PartitionSpec as P

WINDOW = 4
MP = 4
PER = 2
QTOK = 32
PTOK = 180
DIM = 128
ROWS = PER * PTOK
OWN = PER * QTOK
BLK = MP * OWN
SPAN = 2 * WINDOW - 1
NEG = -1e30
ROOT = DIM ** (-0.5)
MESH = pl.DeviceIdType.MESH
F32 = jnp.float32
BF16 = jnp.bfloat16


def spread_pairs(x):
    x = x + pltpu.roll(x, 4, 0)
    return x + pltpu.roll(x, 2, 0)


def max_pairs(x):
    x = jnp.maximum(x, pltpu.roll(x, 4, 0))
    return jnp.maximum(x, pltpu.roll(x, 2, 0))


def token_sum(x, same):
    hi = x.astype(BF16)
    rest = x - hi.astype(F32)
    mid = rest.astype(BF16)
    low = (rest - mid.astype(F32)).astype(BF16)
    dot = functools.partial(jnp.dot, preferred_element_type=F32)
    return dot(hi, same) + (dot(mid, same) + dot(low, same))


def work(
    blocks,
    q_hbm,
    p_hbm,
    len_ref,
    pos_ref,
    loss_ref,
    qg_ref,
    pg_ref,
    qall,
    p_ref,
    pcat,
    w_ref,
    gsend,
    grecv,
    sall,
    ctok,
    q_send,
    q_recv,
    s_send,
    s_recv,
    g_send,
    g_recv,
    local,
):
    b = lax.axis_index("blk")
    m = lax.axis_index("mp")

    def block(d):
        return lax.rem(b + (d + blocks), blocks)

    def lane(k):
        return lax.rem(m + k, MP)

    def remote(src, dst, send, recv, d, k):
        return pltpu.make_async_remote_copy(
            src_ref=src,
            dst_ref=dst,
            send_sem=send,
            recv_sem=recv,
            device_id={"blk": block(d), "mp": lane(k)},
            device_id_type=MESH,
        )

    barrier = pltpu.get_barrier_semaphore()
    near = [
        (d, k)
        for d in (3, 2, 1, -1, -2, -3, 0)
        for k in range(MP)
        if not (d == 0 and k == 0)
    ]
    for d, k in near:
        pl.semaphore_signal(
            barrier, inc=1, device_id={"blk": block(d), "mp": lane(k)}, device_id_type=MESH
        )
    own_q = pltpu.make_async_copy(q_hbm, qall.at[m], local.at[0])
    own_q.start()
    own_p = pltpu.make_async_copy(p_hbm, p_ref, local.at[1])
    own_p.start()

    row8 = lax.broadcasted_iota(jnp.int32, (8, BLK), 0)
    lane8 = lax.broadcasted_iota(jnp.int32, (8, BLK), 1)
    parity = row8 % 2
    group = row8 // 2
    lens = jnp.where(parity == 0, len_ref[0], len_ref[1])
    log_len = jnp.log(lens.astype(F32)) * QTOK
    query_of = lane8 // QTOK
    pos = jnp.zeros((8, BLK), jnp.int32)
    for n in range(MP * PER):
        pos = jnp.where(query_of == n, pos_ref[0, n], pos)
    same = (
        lax.broadcasted_iota(jnp.int32, (BLK, BLK), 0) // QTOK
        == lax.broadcasted_iota(jnp.int32, (BLK, BLK), 1) // QTOK
    ).astype(F32).astype(BF16)

    pl.semaphore_wait(barrier, len(near))
    waits = []
    for s in (3, 2, 1, 0):
        for k in range(MP):
            if s == 0 and k == 0:
                continue
            c = remote(
                q_hbm, qall.at[s * MP + m], q_send.at[s * MP + k], q_recv.at[s * MP + m], s, k
            )
            c.start()
            waits.append(c)

    own_p.wait()
    p_rows = p_ref[...]
    p32 = p_rows.astype(F32)
    odd = lax.broadcasted_iota(jnp.int32, (ROWS, DIM), 0) % 2
    pcat[:, :DIM] = jnp.where(odd == 0, p32, 0.0).astype(BF16)
    pcat[:, DIM:] = jnp.where(odd == 1, p32, 0.0).astype(BF16)
    token = (
        lax.broadcasted_iota(jnp.int32, (ROWS // 8, 8, BLK), 0) * 4
        + lax.broadcasted_iota(jnp.int32, (ROWS // 8, 8, BLK), 1) // 2
    )
    live = token < lens[None]

    own_q.wait()
    message = jnp.zeros((8, BLK), F32)
    for s in range(WINDOW):
        for k in range(MP):
            if s == 0 and k == 0:
                continue
            i = s * MP + lane(k)
            remote(q_hbm, qall.at[i], q_send.at[0], q_recv.at[i], s, k).wait_recv()
        q_blk = qall[s * MP : (s + 1) * MP].reshape(BLK, DIM)
        logits = lax.dot_general(
            p_rows, q_blk, (((1,), (1,)), ((), ())), preferred_element_type=F32
        ).reshape(ROWS // 8, 8, BLK)
        logits = jnp.where(live, logits, NEG)
        top = max_pairs(jnp.max(logits, axis=0))
        terms = jnp.exp2((logits - top[None]) * (ROOT * math.log2(math.e)))
        total = spread_pairs(jnp.sum(terms, axis=0))
        w_ref[s] = (terms * (1.0 / total)[None]).reshape(ROWS, BLK)
        score = token_sum(top * ROOT + jnp.log(total), same) - log_len
        message = jnp.where(group == s, score, message)

    sall[(WINDOW - 1) * MP + m] = message
    mine = (WINDOW - 1) * MP + m
    for d in (3, -3, 2, -2, 1, -1, 0):
        for k in range(MP):
            if d == 0 and k == 0:
                continue
            i = (WINDOW - 1 - d) * MP + m
            c = remote(
                sall.at[mine],
                sall.at[i],
                s_send.at[(d + WINDOW - 1) * MP + k],
                s_recv.at[i],
                d,
                k,
            )
            c.start()
            waits.append(c)

    for s in range(WINDOW):
        w = w_ref[s]
        hi = w.astype(BF16)
        low = (w - hi.astype(F32)).astype(BF16)
        over_rows = functools.partial(
            lax.dot_general,
            dimension_numbers=(((0,), (0,)), ((), ())),
            preferred_element_type=F32,
        )
        g = over_rows(hi, pcat[...]) + over_rows(low, pcat[...])
        gsend[s] = g.astype(BF16).reshape(MP, OWN, PER * DIM)
        for k in range(MP):
            if s == 0 and k == 0:
                continue
            c = remote(
                gsend.at[s, lane(k)],
                grecv.at[s * MP + m],
                g_send.at[s * MP + k],
                g_recv.at[s * MP + m],
                -s,
                k,
            )
            c.start()
            waits.append(c)
    grecv[m] = gsend[0, m]

    for d in range(1 - WINDOW, WINDOW):
        for k in range(MP):
            if d == 0 and k == 0:
                continue
            i = (d + WINDOW - 1) * MP + lane(k)
            remote(sall.at[mine], sall.at[i], s_send.at[0], s_recv.at[i], 0, k).wait_recv()

    tops = []
    for d in range(1 - WINDOW, WINDOW):
        t = jnp.max(sall[(d + WINDOW - 1) * MP : (d + WINDOW) * MP], axis=0)
        t = pltpu.roll(t, (-2 * d) % 8, 0) if d else t
        tops.append(jnp.where((group + d >= 0) & (group + d < WINDOW), t, NEG))
    top = functools.reduce(jnp.maximum, tops)
    top = jnp.maximum(
        top, jnp.where(parity == 0, pltpu.roll(top, 7, 0), pltpu.roll(top, 1, 0))
    )
    total = jnp.zeros((8, BLK), F32)
    for d in range(1 - WINDOW, WINDOW):
        there = pltpu.roll(top, (2 * d) % 8, 0) if d else top
        inside = (group - d >= 0) & (group - d < WINDOW)
        tile = sall[(d + WINDOW - 1) * MP : (d + WINDOW) * MP]
        t = jnp.sum(jnp.exp(jnp.where(inside[None], tile - there[None], NEG)), axis=0)
        total = total + (pltpu.roll(t, (-2 * d) % 8, 0) if d else t)
    total = total + jnp.where(
        parity == 0, pltpu.roll(total, 7, 0), pltpu.roll(total, 1, 0)
    )
    lse = top + jnp.log(total)

    first = group == 0
    hit = jnp.where(first & (pos == PER * m + parity), 1.0, 0.0)
    coef = jnp.exp(sall[mine] - lse) - hit
    pg = jnp.zeros((ROWS, DIM), F32)
    for s in range(WINDOW):
        c = spread_pairs(jnp.where(group == s, coef, 0.0))
        d_rows = (w_ref[s].reshape(ROWS // 8, 8, BLK) * c[None]).reshape(ROWS, BLK)
        q_blk = qall[s * MP : (s + 1) * MP].reshape(BLK, DIM)
        pg = pg + jnp.dot(d_rows.astype(BF16), q_blk, preferred_element_type=F32)
    pg_ref[...] = pg * ROOT

    lse_own = jnp.broadcast_to(lse[0:1], (8, BLK))
    found = jnp.zeros((8, BLK), F32)
    parts = []
    for k in range(MP):
        t = jnp.zeros((8, BLK), F32)
        for d in range(WINDOW):
            t = jnp.where(group == d, sall[(d + WINDOW - 1) * MP + k], t)
        here = first & (pos == PER * k + parity)
        found = jnp.where(here, t, found)
        parts.append(jnp.exp(t - lse_own) - jnp.where(here, 1.0, 0.0))
    parts.append(jnp.zeros((DIM - 8 * MP, BLK), F32))
    ctok[...] = jnp.concatenate(parts, axis=0).T
    loss = lse_own - jnp.broadcast_to(jnp.sum(found, axis=0, keepdims=True), (8, BLK))
    one = [
        jnp.sum(jnp.where(lane8[0:1] == m * OWN + n * QTOK, loss[0:1], 0.0)) for n in range(PER)
    ]
    place = lax.broadcasted_iota(jnp.int32, (1, PER), 1)
    loss_ref[...] = jnp.where(place == 0, one[0], one[1])

    for s in range(WINDOW):
        for k in range(MP):
            if s == 0 and k == 0:
                continue
            i = s * MP + lane(k)
            remote(gsend.at[0, 0], grecv.at[i], g_send.at[0], g_recv.at[i], 0, k).wait_recv()
    mine_tok = ctok[pl.ds(pl.multiple_of(m * OWN, OWN), OWN), :]
    qg = jnp.zeros((OWN, DIM), F32)
    for k in range(MP):
        for s in range(WINDOW):
            for p in range(PER):
                col = 8 * k + 2 * s + p
                g = grecv[s * MP + k, :, p * DIM : (p + 1) * DIM].astype(F32)
                qg = qg + mine_tok[:, col : col + 1] * g
    qg_ref[...] = qg * ROOT
    for c in waits:
        c.wait_send()


def store(loss_ref, qg_ref, pg_ref, loss_out, qg_out, pg_out, sems):
    copies = [
        pltpu.make_async_copy(src, dst, sems.at[i])
        for i, (src, dst) in enumerate(
            ((pg_ref, pg_out), (qg_ref, qg_out), (loss_ref, loss_out))
        )
    ]
    for c in copies:
        c.start()
    for c in copies:
        c.wait()


def on_device(blocks, queries, passages, lengths, pos_index):
    hbm = pl.BlockSpec(memory_space=pl.ANY)
    vmem = pl.BlockSpec(memory_space=pltpu.VMEM)
    smem = pl.BlockSpec(memory_space=pltpu.SMEM)
    shapes = ((1, PER), (OWN, DIM), (ROWS, DIM))
    slots = WINDOW * MP
    dma = pltpu.SemaphoreType.DMA
    results = pl.pallas_call(
        functools.partial(work, blocks),
        out_shape=tuple(pltpu.VMEM(s, F32) for s in shapes),
        in_specs=[hbm, hbm, smem, smem],
        out_specs=(vmem,) * 3,
        scratch_shapes=[
            pltpu.VMEM((slots, OWN, DIM), BF16),
            pltpu.VMEM((ROWS, DIM), BF16),
            pltpu.VMEM((ROWS, PER * DIM), BF16),
            pltpu.VMEM((WINDOW, ROWS, BLK), F32),
            pltpu.VMEM((WINDOW, MP, OWN, PER * DIM), BF16),
            pltpu.VMEM((slots, OWN, PER * DIM), BF16),
            pltpu.VMEM((SPAN * MP, 8, BLK), F32),
            pltpu.VMEM((BLK, DIM), F32),
            dma((slots,)),
            dma((slots,)),
            dma((SPAN * MP,)),
            dma((SPAN * MP,)),
            dma((slots,)),
            dma((slots,)),
            dma((2,)),
        ],
        compiler_params=pltpu.CompilerParams(
            collective_id=0, has_side_effects=True, vmem_limit_bytes=24 * 1024 * 1024
        ),
    )(
        queries.reshape(OWN, DIM),
        passages.transpose(1, 0, 2).reshape(ROWS, DIM),
        lengths,
        pos_index,
    )
    loss, qg, pg = pl.pallas_call(
        store,
        out_shape=tuple(jax.ShapeDtypeStruct(s, F32) for s in shapes),
        in_specs=[vmem] * 3,
        out_specs=(hbm,) * 3,
        scratch_shapes=[dma((3,))],
    )(*results)
    return (
        loss.reshape(PER),
        qg.reshape(PER, QTOK, DIM),
        pg.reshape(PTOK, PER, DIM).transpose(1, 0, 2),
    )


def solution(mesh):
    placed = (
        P(("blk", "mp"), None, None),
        P(("blk", "mp"), None, None),
        P(("blk", "mp")),
        P("blk", None),
    )
    return jax.shard_map(
        functools.partial(on_device, mesh.shape["blk"]),
        mesh=mesh,
        in_specs=placed,
        out_specs=(P(("blk", "mp")), P(("blk", "mp"), None, None), P(("blk", "mp"), None, None)),
        check_vma=False,
    )
```

time: 249 us -> 59.4 us (0.24)
  the two profiles are of different devices: /device:TPU:1 before, /device:TPU:8 now
where the time goes in v1:
time: 59.4 us; the launch traced here: 59.2 us
  Pallas kernels  54.4 us (92%)
  local copies, waits for them, and re-layouts  4.07 us (7%)
  between operations  0.67 us (1%)
    pallas_call x1, Pallas kernels, on_device(): pl.pallas_call(functools.partial(work, blocks), out_shape=tuple((pltpu.VM...  52.8 us
    unnamed x14, local copies, waits for them, and re-layouts  4.07 us
    pallas_call x1, Pallas kernels, on_device(): pl.pallas_call(store, out_shape=tuple((jax.ShapeDtypeStruct(s, F32) for s...  1.65 us

profile of v1, /device:TPU:8, one launch (start us, length us, event | category | flops | bytes accessed | tf_op | source)
XLA Modules:
  0.0 59.2 jit_solution(7131118454717056054)
XLA Ops:
  0.6 0.0 copy-start.4
  0.6 0.0 copy-start.5
  0.7 0.6 %copy-done.4 = s32[2]{0:T(128)S(1)} copy-done((s32[2]{0:T(128)S(1)}, s32[2]{0:T(128)}, u32[]{:S(2)}) %copy-start.4) | copy-done | bytes 32
  1.3 0.0 copy-done.5
  1.3 0.0 copy-start.1
  1.3 0.9 %copy-done.1 = bf16[2,180,128]{2,0,1:T(2,128)(2,1)S(1)} copy-done((bf16[2,180,128]{2,0,1:T(2,128)(2,1)S(1)}, bf16[2,180,128]{2,0,1:T(2,128)(2,1)}, u32[]{:S(2)}) %copy-start.1) | copy-done | bytes 92184
  2.2 0.0 copy-start.3
  2.2 0.7 %copy-done.3 = bf16[2,32,128]{2,1,0:T(8,128)(2,1)S(1)} copy-done((bf16[2,32,128]{2,1,0:T(8,128)(2,1)S(1)}, bf16[2,32,128]{2,1,0:T(8,128)(2,1)}, u32[]{:S(2)}) %copy-start.3) | copy-done | bytes 16408
  2.9 52.8 %shard_map.67 = (f32[1,2]{1,0:T(1,128)S(1)}, f32[64,128]{1,0:T(8,128)S(1)}, f32[360,128]{1,0:T(8,128)S(1)}) custom-call(bf16[64,128]{1,0:T(8,128)(2,1)S(1)} %bitcast.10, bf16[360,128]{1,0:T(8,128)(2,1)S(1)} %bitcast.9, s32[2]{0:T(128)S(1)} %copy-done.4, s32[1,8]{1,0:T(1,128)S(1)} %copy-done.5), custom_call_target="tpu_custom_call" | custom-call | tf_op jit(solution)/shard_map/pallas_call | solution.py:307
  55.7 0.0 copy-start
  55.7 0.7 %copy-done = f32[360,128]{1,0:T(8,128)} copy-done((f32[360,128]{1,0:T(8,128)}, f32[360,128]{1,0:T(8,128)S(1)}, u32[]{:S(2)}) %copy-start) | copy-done | bytes 184344
  56.4 0.0 copy-start.2
  56.4 0.6 %copy-done.2 = f32[64,128]{1,0:T(8,128)} copy-done((f32[64,128]{1,0:T(8,128)}, f32[64,128]{1,0:T(8,128)S(1)}, u32[]{:S(2)}) %copy-start.2) | copy-done | bytes 32792
  57.0 0.0 copy-start.6
  57.0 0.5 copy-done.6
  57.5 1.6 %shard_map.68 = (f32[1,2]{1,0:T(1,128)}, f32[64,128]{1,0:T(8,128)}, f32[360,128]{1,0:T(8,128)}) custom-call(f32[1,2]{1,0:T(1,128)} %copy-done.6, f32[64,128]{1,0:T(8,128)} %copy-done.2, f32[360,128]{1,0:T(8,128)} %copy-done), custom_call_target="tpu_custom_call" | custom-call | tf_op jit(solution)/shard_map/pallas_call | solution.py:338
Async XLA Ops:
  0.6 0.7 %copy-start.4 = (s32[2]{0:T(128)S(1)}, s32[2]{0:T(128)}, u32[]{:S(2)}) copy-start(s32[2]{0:T(128)} %len_ref.1) | copy-start | bytes 28
  0.6 0.7 %copy-start.5 = (s32[1,8]{1,0:T(1,128)S(1)}, s32[1,8]{1,0:T(1,128)}, u32[]{:S(2)}) copy-start(s32[1,8]{1,0:T(1,128)} %pos_ref.1) | copy-start | bytes 100
  1.3 0.9 %copy-start.1 = (bf16[2,180,128]{2,0,1:T(2,128)(2,1)S(1)}, bf16[2,180,128]{2,0,1:T(2,128)(2,1)}, u32[]{:S(2)}) copy-start(bf16[2,180,128]{2,0,1:T(2,128)(2,1)} %param.5) | copy-start | bytes 276484
  2.2 0.7 %copy-start.3 = (bf16[2,32,128]{2,1,0:T(8,128)(2,1)S(1)}, bf16[2,32,128]{2,1,0:T(8,128)(2,1)}, u32[]{:S(2)}) copy-start(bf16[2,32,128]{2,1,0:T(8,128)(2,1)} %param.4) | copy-start | bytes 49156
  55.7 0.7 %copy-start = (f32[360,128]{1,0:T(8,128)}, f32[360,128]{1,0:T(8,128)S(1)}, u32[]{:S(2)}) copy-start(f32[360,128]{1,0:T(8,128)S(1)} %get-tuple-element.11.pg_ref) | copy-start | bytes 552964
  56.4 0.6 %copy-start.2 = (f32[64,128]{1,0:T(8,128)}, f32[64,128]{1,0:T(8,128)S(1)}, u32[]{:S(2)}) copy-start(f32[64,128]{1,0:T(8,128)S(1)} %get-tuple-element.10.qg_ref) | copy-start | bytes 98308
  57.0 0.5 copy-start.6

commit v2 on v1

v2 whole, which is shorter than its diff:
```python
import functools
import math

import jax
import jax.numpy as jnp
from jax import lax
from jax.experimental import pallas as pl
from jax.experimental.pallas import tpu as pltpu
from jax.sharding import PartitionSpec as P

WINDOW = 4
SIDES = 2
CORES = 2
PER = 2
QTOK = 32
PTOK = 180
DIM = 128
ROWS = PER * PTOK
TILES = ROWS // 8
OWN = PER * QTOK
BLK = SIDES * OWN
RING_X = 4
LAYER = 32
NEG = -1e30
ROOT = DIM ** (-0.5)
MESH = pl.DeviceIdType.MESH
F32 = jnp.float32
BF16 = jnp.bfloat16


def spread_pairs(x):
    x = x + pltpu.roll(x, 4, 0)
    return x + pltpu.roll(x, 2, 0)


def max_pairs(x):
    x = jnp.maximum(x, pltpu.roll(x, 4, 0))
    return jnp.maximum(x, pltpu.roll(x, 2, 0))


def token_sum(x, same):
    hi = x.astype(BF16)
    rest = x - hi.astype(F32)
    mid = rest.astype(BF16)
    low = (rest - mid.astype(F32)).astype(BF16)
    dot = functools.partial(jnp.dot, preferred_element_type=F32)
    return dot(hi, same) + (dot(mid, same) + dot(low, same))


def work(
    blocks,
    q_hbm,
    p_hbm,
    len_hbm,
    pos_hbm,
    loss_ref,
    qg_ref,
    pg_ref,
    qall,
    p_ref,
    w_ref,
    msg_ref,
    sall,
    lens_ref,
    gsend,
    grecv,
    pgacc,
    pgrecv,
    lse_ref,
    len_ref,
    pos_ref,
    q_send,
    q_recv,
    s_send,
    s_recv,
    g_send,
    g_recv,
    pair_send,
    pair_recv,
    local,
):
    b = lax.axis_index("blk")
    m = lax.axis_index("mp")
    y = m // CORES
    core = m % CORES
    other = 1 - core

    def block(d):
        return lax.rem(b + (d + blocks), blocks)

    def remote(src, dst, send, recv, d, side, who):
        return pltpu.make_async_remote_copy(
            src_ref=src,
            dst_ref=dst,
            send_sem=send,
            recv_sem=recv,
            device_id={"blk": block(d), "mp": side * CORES + who},
            device_id_type=MESH,
        )

    def send_queries(s, k):
        side = (y + k) % SIDES
        return remote(
            q_hbm, qall.at[s, y], q_send.at[s * SIDES + k], q_recv.at[s * SIDES + y], s, side, core
        )

    def send_scores(s, t, k):
        side = (y + k) % SIDES
        return remote(
            msg_ref.at[s],
            sall.at[t, s * SIDES + y],
            s_send.at[(s * WINDOW + t) * SIDES + k],
            s_recv.at[(t * WINDOW + s) * SIDES + y],
            t - s,
            side,
            core,
        )

    def send_grads(s, k):
        side = (y + k) % SIDES
        return remote(
            gsend.at[s, side],
            grecv.at[s * SIDES + y],
            g_send.at[s * SIDES + k],
            g_recv.at[s * SIDES + y],
            -s,
            side,
            core,
        )

    barrier = pltpu.get_barrier_semaphore()
    near = [
        (d, k) for d in (3, 2, 1, -1, -2, -3, 0) for k in range(SIDES) if not (d == 0 and k == 0)
    ]
    for d, k in near:
        pl.semaphore_signal(
            barrier,
            inc=1,
            device_id={"blk": block(d), "mp": (y + k) % SIDES * CORES + core},
            device_id_type=MESH,
        )
    pl.semaphore_signal(
        barrier, inc=1, device_id={"blk": b, "mp": y * CORES + other}, device_id_type=MESH
    )
    get_len = pltpu.make_async_copy(len_hbm, len_ref, local.at[0])
    get_len.start()
    get_pos = pltpu.make_async_copy(pos_hbm, pos_ref, local.at[1])
    get_pos.start()
    get_q = pltpu.make_async_copy(q_hbm, qall.at[0, y], local.at[2])
    get_q.start()
    get_p = pltpu.make_async_copy(p_hbm, p_ref.at[core], local.at[3])
    get_p.start()
    pl.semaphore_wait(barrier, len(near) + 1)

    for s in (3, 2, 1, 0):
        for k in range(SIDES):
            if s or k:
                send_queries(s, k).start()
    pair_p = remote(p_hbm, p_ref.at[core], pair_send.at[0], pair_recv.at[0], 0, y, other)
    pair_p.start()

    row8 = lax.broadcasted_iota(jnp.int32, (8, BLK), 0)
    lane8 = lax.broadcasted_iota(jnp.int32, (8, BLK), 1)
    parity = row8 % 2
    half = row8 // 2 % 2
    get_len.wait()
    lens_ref[core] = jnp.where(parity == 0, len_ref[0], len_ref[1]).astype(F32)
    pair_len = remote(
        lens_ref.at[core], lens_ref.at[core], pair_send.at[1], pair_recv.at[1], 0, y, other
    )
    pair_len.start()
    get_pos.wait()
    query_of = lane8 // QTOK
    pos = jnp.zeros((8, BLK), jnp.int32)
    for side in range(SIDES):
        for i in range(PER):
            n = side * CORES * PER + core * PER + i
            pos = jnp.where(query_of == side * PER + i, pos_ref[0, n], pos)
    same = (
        lax.broadcasted_iota(jnp.int32, (BLK, BLK), 0) // QTOK
        == lax.broadcasted_iota(jnp.int32, (BLK, BLK), 1) // QTOK
    ).astype(F32).astype(BF16)
    token = (
        lax.broadcasted_iota(jnp.int32, (TILES, 8, BLK), 0) * 4
        + lax.broadcasted_iota(jnp.int32, (TILES, 8, BLK), 1) // 2
    )
    pgacc[...] = jnp.zeros_like(pgacc)
    get_p.wait()
    get_q.wait()
    pair_p.wait_recv()
    pair_len.wait_recv()

    def score_block(s, _):
        def arrived(side):
            remote(
                q_hbm, qall.at[s, side], q_send.at[0], q_recv.at[s * SIDES + side], 0, side, core
            ).wait_recv()

        arrived(1 - y)

        @pl.when(s > 0)
        def _():
            arrived(y)

        q_blk = qall[s].reshape(BLK, DIM)
        scores = []
        for h in range(CORES):
            logits = lax.dot_general(
                p_ref[h], q_blk, (((1,), (1,)), ((), ())), preferred_element_type=F32
            ).reshape(TILES, 8, BLK)
            lens = lens_ref[h]
            logits = jnp.where(token < lens.astype(jnp.int32)[None], logits, NEG)
            top = max_pairs(jnp.max(logits, axis=0))
            terms = jnp.exp2((logits - top[None]) * (ROOT * math.log2(math.e)))
            total = spread_pairs(jnp.sum(terms, axis=0))
            w_ref[s, h] = terms * (1.0 / total)[None]
            scores.append(token_sum(top * ROOT + jnp.log(total), same) - jnp.log(lens) * QTOK)
        message = jnp.where(half == 0, scores[0], scores[1])
        msg_ref[s] = message
        sall[s, s * SIDES + y] = message
        for u in range(WINDOW):
            t = (s + 1 + u) % WINDOW
            send_scores(s, t, 1).start()
            if u < WINDOW - 1:
                send_scores(s, t, 0).start()
        return 0

    def grad_block(s, _):
        for j in range(WINDOW):
            for side in range(SIDES):

                @pl.when((s != j) | (y != side))
                def _():
                    remote(
                        msg_ref.at[0],
                        sall.at[s, j * SIDES + side],
                        s_send.at[0],
                        s_recv.at[(s * WINDOW + j) * SIDES + side],
                        0,
                        side,
                        core,
                    ).wait_recv()

        tile = sall[s]
        top = jnp.max(tile, axis=0)
        top = jnp.maximum(top, pltpu.roll(top, 1, 0))
        top = jnp.maximum(top, pltpu.roll(top, 2, 0))
        total = jnp.sum(jnp.exp(tile - top[None]), axis=0)
        total = total + pltpu.roll(total, 1, 0)
        total = total + pltpu.roll(total, 2, 0)
        lse = top + jnp.log(total)
        lse_ref[s] = lse
        here = (pos == y * (CORES * PER) + row8 % (CORES * PER)) & (s == 0)
        coef = jnp.exp(msg_ref[s] - lse) - jnp.where(here, 1.0, 0.0)
        turned = pltpu.roll(coef, 2, 0)
        q_blk = qall[s].reshape(BLK, DIM)
        dq = jnp.zeros((BLK, DIM), F32)
        rows = []
        for h in range(CORES):
            c = jnp.where(half == h, coef, turned)
            d_rows = (w_ref[s, h] * c[None]).reshape(ROWS, BLK).astype(BF16)
            rows.append(d_rows)
            dq = dq + lax.dot_general(
                d_rows, p_ref[h], (((0,), (0,)), ((), ())), preferred_element_type=F32
            )
        gsend[s] = dq.astype(BF16).reshape(SIDES, OWN, DIM)
        send_grads(s, 1).start()

        @pl.when(s > 0)
        def _():
            send_grads(s, 0).start()

        for h in range(CORES):
            pgacc[h] += jnp.dot(rows[h], q_blk, preferred_element_type=F32)
        return 0

    early = jnp.where(b % LAYER < RING_X, b % RING_X + 1, WINDOW)

    def run(g, _):
        low = g * early
        high = early + g * (WINDOW - early)
        lax.fori_loop(low, high, score_block, 0)
        lax.fori_loop(low, high, grad_block, 0)
        return 0

    lax.fori_loop(0, 2, run, 0)

    pair_pg = remote(pgacc.at[other], pgrecv, pair_send.at[2], pair_recv.at[2], 0, y, other)
    pair_pg.start()

    found = jnp.zeros((8, BLK), F32)
    for side in range(SIDES):
        here = (pos == side * (CORES * PER) + row8) & (row8 < CORES * PER)
        found = found + jnp.where(here, sall[0, side], 0.0)
    loss = lse_ref[0][0:1] - jnp.sum(found, axis=0, keepdims=True)
    one = [
        jnp.sum(jnp.where(lane8[0:1] == y * OWN + n * QTOK, loss, 0.0)) for n in range(PER)
    ]
    place = lax.broadcasted_iota(jnp.int32, (1, PER), 1)
    loss_ref[...] = jnp.where(place == 0, one[0], one[1])

    qg = gsend[0, y].astype(F32)
    for s in range(WINDOW):
        for k in range(SIDES):
            if s or k:
                i = s * SIDES + (y + k) % SIDES
                remote(
                    gsend.at[0, 0], grecv.at[i], g_send.at[0], g_recv.at[i], 0, y, core
                ).wait_recv()
                qg = qg + grecv[i].astype(F32)
    qg_ref[...] = qg * ROOT
    pair_pg.wait_recv()
    pg_ref[...] = (pgacc[core] + pgrecv[...]) * ROOT

    pair_p.wait_send()
    pair_len.wait_send()
    pair_pg.wait_send()
    for s in range(WINDOW):
        for k in range(SIDES):
            if s or k:
                send_queries(s, k).wait_send()
                send_grads(s, k).wait_send()
            for t in range(WINDOW):
                if s != t or k:
                    send_scores(s, t, k).wait_send()


def store(loss_ref, qg_ref, pg_ref, loss_out, qg_out, pg_out, sems):
    copies = [
        pltpu.make_async_copy(src, dst, sems.at[i])
        for i, (src, dst) in enumerate(
            ((pg_ref, pg_out), (qg_ref, qg_out), (loss_ref, loss_out))
        )
    ]
    for c in copies:
        c.start()
    for c in copies:
        c.wait()


def on_device(blocks, queries, passages, lengths, pos_index):
    hbm = pl.BlockSpec(memory_space=pltpu.HBM)
    vmem = pl.BlockSpec(memory_space=pltpu.VMEM)
    shapes = ((1, PER), (OWN, DIM), (ROWS, DIM))
    slots = WINDOW * SIDES
    dma = pltpu.SemaphoreType.DMA
    operands = (
        queries.reshape(OWN, DIM),
        passages.transpose(1, 0, 2).reshape(ROWS, DIM),
        lengths,
        pos_index,
    )
    results = pl.pallas_call(
        functools.partial(work, blocks),
        out_shape=tuple(pltpu.VMEM(s, F32) for s in shapes),
        in_specs=[hbm] * 4,
        out_specs=(vmem,) * 3,
        scratch_shapes=[
            pltpu.VMEM((WINDOW, SIDES, OWN, DIM), BF16),
            pltpu.VMEM((CORES, ROWS, DIM), BF16),
            pltpu.VMEM((WINDOW, CORES, TILES, 8, BLK), F32),
            pltpu.VMEM((WINDOW, 8, BLK), F32),
            pltpu.VMEM((WINDOW, slots, 8, BLK), F32),
            pltpu.VMEM((CORES, 8, BLK), F32),
            pltpu.VMEM((WINDOW, SIDES, OWN, DIM), BF16),
            pltpu.VMEM((slots, OWN, DIM), BF16),
            pltpu.VMEM((CORES, ROWS, DIM), F32),
            pltpu.VMEM((ROWS, DIM), F32),
            pltpu.VMEM((WINDOW, 8, BLK), F32),
            pltpu.SMEM((PER,), jnp.int32),
            pltpu.SMEM((1, WINDOW * PER), jnp.int32),
            dma((slots,)),
            dma((slots,)),
            dma((WINDOW * slots,)),
            dma((WINDOW * slots,)),
            dma((slots,)),
            dma((slots,)),
            dma((3,)),
            dma((3,)),
            dma((4,)),
        ],
        compiler_params=pltpu.CompilerParams(
            collective_id=0, has_side_effects=True, vmem_limit_bytes=24 * 1024 * 1024
        ),
    )(*(pltpu.with_memory_space_constraint(x, pltpu.HBM) for x in operands))
    loss, qg, pg = pl.pallas_call(
        store,
        out_shape=tuple(pltpu.HBM(s, F32) for s in shapes),
        in_specs=[vmem] * 3,
        out_specs=(hbm,) * 3,
        scratch_shapes=[dma((3,))],
    )(*results)
    return (
        loss.reshape(PER),
        qg.reshape(PER, QTOK, DIM),
        pg.reshape(PTOK, PER, DIM).transpose(1, 0, 2),
    )


def solution(mesh):
    placed = (
        P(("blk", "mp"), None, None),
        P(("blk", "mp"), None, None),
        P(("blk", "mp")),
        P("blk", None),
    )
    return jax.shard_map(
        functools.partial(on_device, mesh.shape["blk"]),
        mesh=mesh,
        in_specs=placed,
        out_specs=(P(("blk", "mp")), P(("blk", "mp"), None, None), P(("blk", "mp"), None, None)),
        check_vma=False,
    )
```

time: 59.4 us -> 41.3 us (0.70)
  the two profiles are of different devices: /device:TPU:8 before, /device:TPU:1 now
where the time goes in v2:
time: 41.3 us; the launch traced here: 41.1 us
  Pallas kernels  38.6 us (93%)
  local copies, waits for them, and re-layouts  1.86 us (5%)
  between operations  0.65 us (2%)
    pallas_call x1, Pallas kernels, on_device(): pl.pallas_call(functools.partial(work, blocks), out_shape=tuple((pltpu.VM...  37 us
    unnamed x6, local copies, waits for them, and re-layouts  1.86 us
    pallas_call x1, Pallas kernels, on_device(): pl.pallas_call(store, out_shape=tuple((pltpu.HBM(s, F32) for s in shapes)...  1.65 us

profile of v2, /device:TPU:1, one launch (start us, length us, event | category | flops | bytes accessed | tf_op | source)
XLA Modules:
  0.0 41.1 jit_solution(4919436283486526681)
XLA Ops:
  0.6 37.0 %shard_map.67 = (f32[1,2]{1,0:T(1,128)S(1)}, f32[64,128]{1,0:T(8,128)S(1)}, f32[360,128]{1,0:T(8,128)S(1)}) custom-call(bf16[64,128]{1,0:T(8,128)(2,1)} %bitcast.10, bf16[360,128]{1,0:T(8,128)(2,1)} %bitcast.9, s32[2]{0:T(128)} %len_hbm.1, s32[1,8]{1,0:T(1,128)} %pos_hbm.1), custom_call_target="tpu_custom_call" | custom-call | tf_op jit(solution)/shard_map/pallas_call | solution.py:353
  37.6 0.0 copy-start
  37.6 0.7 %copy-done = f32[360,128]{1,0:T(8,128)} copy-done((f32[360,128]{1,0:T(8,128)}, f32[360,128]{1,0:T(8,128)S(1)}, u32[]{:S(2)}) %copy-start) | copy-done | bytes 184344
  38.3 0.0 copy-start.1
  38.3 0.6 %copy-done.1 = f32[64,128]{1,0:T(8,128)} copy-done((f32[64,128]{1,0:T(8,128)}, f32[64,128]{1,0:T(8,128)S(1)}, u32[]{:S(2)}) %copy-start.1) | copy-done | bytes 32792
  38.9 0.0 copy-start.2
  38.9 0.6 %copy-done.2 = f32[1,2]{1,0:T(1,128)} copy-done((f32[1,2]{1,0:T(1,128)}, f32[1,2]{1,0:T(1,128)S(1)}, u32[]{:S(2)}) %copy-start.2) | copy-done | bytes 32
  39.5 1.6 %shard_map.68 = (f32[1,2]{1,0:T(1,128)}, f32[64,128]{1,0:T(8,128)}, f32[360,128]{1,0:T(8,128)}) custom-call(f32[1,2]{1,0:T(1,128)} %copy-done.2, f32[64,128]{1,0:T(8,128)} %copy-done.1, f32[360,128]{1,0:T(8,128)} %copy-done), custom_call_target="tpu_custom_call" | custom-call | tf_op jit(solution)/shard_map/pallas_call | solution.py:386
Async XLA Ops:
  37.6 0.7 %copy-start = (f32[360,128]{1,0:T(8,128)}, f32[360,128]{1,0:T(8,128)S(1)}, u32[]{:S(2)}) copy-start(f32[360,128]{1,0:T(8,128)S(1)} %get-tuple-element.11.pg_ref) | copy-start | bytes 552964
  38.3 0.6 %copy-start.1 = (f32[64,128]{1,0:T(8,128)}, f32[64,128]{1,0:T(8,128)S(1)}, u32[]{:S(2)}) copy-start(f32[64,128]{1,0:T(8,128)S(1)} %get-tuple-element.10.qg_ref) | copy-start | bytes 98308
  38.9 0.6 %copy-start.2 = (f32[1,2]{1,0:T(1,128)}, f32[1,2]{1,0:T(1,128)S(1)}, u32[]{:S(2)}) copy-start(f32[1,2]{1,0:T(1,128)S(1)} %get-tuple-element.9.loss_ref) | copy-start | bytes 28

commit v3 on v2

--- a/solution.py
+++ b/solution.py
@@ -66,6 +66,7 @@
     grecv,
     pgacc,
     pgrecv,
+    d_ref,
     lse_ref,
     len_ref,
     pos_ref,
@@ -129,9 +130,7 @@
         )
 
     barrier = pltpu.get_barrier_semaphore()
-    near = [
-        (d, k) for d in (3, 2, 1, -1, -2, -3, 0) for k in range(SIDES) if not (d == 0 and k == 0)
-    ]
+    near = [(d, k) for d in (-3, -2, -1, 0) for k in range(SIDES) if d or k]
     for d, k in near:
         pl.semaphore_signal(
             barrier,
@@ -218,11 +217,23 @@
         message = jnp.where(half == 0, scores[0], scores[1])
         msg_ref[s] = message
         sall[s, s * SIDES + y] = message
-        for u in range(WINDOW):
-            t = (s + 1 + u) % WINDOW
-            send_scores(s, t, 1).start()
-            if u < WINDOW - 1:
-                send_scores(s, t, 0).start()
+        send_scores(s, s, 1).start()
+
+        def ahead(t, _):
+            for k in range(SIDES):
+                send_scores(s, t, k).start()
+            return 0
+
+        lax.fori_loop(s + 1, WINDOW, ahead, 0)
+        return 0
+
+    def behind_block(s, _):
+        def behind(t, _):
+            for k in range(SIDES):
+                send_scores(s, t, k).start()
+            return 0
+
+        lax.fori_loop(0, s, behind, 0)
         return 0
 
     def grad_block(s, _):
@@ -254,14 +265,18 @@
         coef = jnp.exp(msg_ref[s] - lse) - jnp.where(here, 1.0, 0.0)
         turned = pltpu.roll(coef, 2, 0)
         q_blk = qall[s].reshape(BLK, DIM)
-        dq = jnp.zeros((BLK, DIM), F32)
-        rows = []
         for h in range(CORES):
             c = jnp.where(half == h, coef, turned)
             d_rows = (w_ref[s, h] * c[None]).reshape(ROWS, BLK).astype(BF16)
-            rows.append(d_rows)
+            d_ref[s, h] = d_rows
+            pgacc[h] += jnp.dot(d_rows, q_blk, preferred_element_type=F32)
+        return 0
+
+    def return_block(s, _):
+        dq = jnp.zeros((BLK, DIM), F32)
+        for h in range(CORES):
             dq = dq + lax.dot_general(
-                d_rows, p_ref[h], (((0,), (0,)), ((), ())), preferred_element_type=F32
+                d_ref[s, h], p_ref[h], (((0,), (0,)), ((), ())), preferred_element_type=F32
             )
         gsend[s] = dq.astype(BF16).reshape(SIDES, OWN, DIM)
         send_grads(s, 1).start()
@@ -270,8 +285,6 @@
         def _():
             send_grads(s, 0).start()
 
-        for h in range(CORES):
-            pgacc[h] += jnp.dot(rows[h], q_blk, preferred_element_type=F32)
         return 0
 
     early = jnp.where(b % LAYER < RING_X, b % RING_X + 1, WINDOW)
@@ -280,13 +293,18 @@
         low = g * early
         high = early + g * (WINDOW - early)
         lax.fori_loop(low, high, score_block, 0)
+        lax.fori_loop(low, high, behind_block, 0)
         lax.fori_loop(low, high, grad_block, 0)
+
+        @pl.when(g == 1)
+        def _():
+            pair_pg.start()
+
+        lax.fori_loop(low, high, return_block, 0)
         return 0
 
+    pair_pg = remote(pgacc.at[other], pgrecv, pair_send.at[2], pair_recv.at[2], 0, y, other)
     lax.fori_loop(0, 2, run, 0)
-
-    pair_pg = remote(pgacc.at[other], pgrecv, pair_send.at[2], pair_recv.at[2], 0, y, other)
-    pair_pg.start()
 
     found = jnp.zeros((8, BLK), F32)
     for side in range(SIDES):
@@ -366,6 +384,7 @@
             pltpu.VMEM((slots, OWN, DIM), BF16),
             pltpu.VMEM((CORES, ROWS, DIM), F32),
             pltpu.VMEM((ROWS, DIM), F32),
+            pltpu.VMEM((WINDOW, CORES, ROWS, BLK), BF16),
             pltpu.VMEM((WINDOW, 8, BLK), F32),
             pltpu.SMEM((PER,), jnp.int32),
             pltpu.SMEM((1, WINDOW * PER), jnp.int32),
@@ -389,7 +408,7 @@
         in_specs=[vmem] * 3,
         out_specs=(hbm,) * 3,
         scratch_shapes=[dma((3,))],
-    )(*results)
+    )(*(pltpu.with_memory_space_constraint(x, pltpu.VMEM) for x in results))
     return (
         loss.reshape(PER),
         qg.reshape(PER, QTOK, DIM),

time: 41.3 us -> 32.3 us (0.78)
  Pallas kernels: 38.6 us -> 31.4 us
  local copies, waits for them, and re-layouts: 1.86 us -> 0 us
    pallas_call x1, Pallas kernels: 37 us -> 30.7 us  [on_device(): pl.pallas_call(functools.partial(work, blocks), out_shape=tuple((pltpu.VM...]
    unnamed x6 -> x0, local copies, waits for them, and re-layouts: 1.86 us -> none
    pallas_call x1, Pallas kernels: 1.65 us -> 0.71 us  [on_device(): pl.pallas_call(store, out_shape=tuple((pltpu.HBM(s, F32) for s in shapes)...]
where the time goes in v3:
time: 32.3 us; the launch traced here: 32 us
  Pallas kernels  31.4 us (97%)
  between operations  0.64 us (2%)
    pallas_call x1, Pallas kernels, on_device(): pl.pallas_call(functools.partial(work, blocks), out_shape=tuple((pltpu.VM...  30.7 us
    pallas_call x1, Pallas kernels, on_device(): pl.pallas_call(store, out_shape=tuple((pltpu.HBM(s, F32) for s in shapes)...  0.71 us

profile of v3, /device:TPU:1, one launch (start us, length us, event | category | flops | bytes accessed | tf_op | source)
XLA Modules:
  0.0 32.0 jit_solution(9760675571009559397)
XLA Ops:
  0.6 30.7 %shard_map.67 = (f32[1,2]{1,0:T(1,128)S(1)}, f32[64,128]{1,0:T(8,128)S(1)}, f32[360,128]{1,0:T(8,128)S(1)}) custom-call(bf16[64,128]{1,0:T(8,128)(2,1)} %bitcast.10, bf16[360,128]{1,0:T(8,128)(2,1)} %bitcast.9, s32[2]{0:T(128)} %len_hbm.1, s32[1,8]{1,0:T(1,128)} %pos_hbm.1), custom_call_target="tpu_custom_call" | custom-call | tf_op jit(solution)/shard_map/pallas_call | solution.py:371
  31.3 0.7 %shard_map.68 = (f32[1,2]{1,0:T(1,128)}, f32[64,128]{1,0:T(8,128)}, f32[360,128]{1,0:T(8,128)}) custom-call(f32[1,2]{1,0:T(1,128)S(1)} %get-tuple-element.9.loss_ref, f32[64,128]{1,0:T(8,128)S(1)} %get-tuple-element.10.qg_ref, f32[360,128]{1,0:T(8,128)S(1)} %get-tuple-element.11.pg_ref), custom_call_target="tpu_custom_call" | custom-call | tf_op jit(solution)/shard_map/pallas_call | solution.py:405

commit v4 on v2

--- a/solution.py
+++ b/solution.py
@@ -43,8 +43,16 @@
     rest = x - hi.astype(F32)
     mid = rest.astype(BF16)
     low = (rest - mid.astype(F32)).astype(BF16)
-    dot = functools.partial(jnp.dot, preferred_element_type=F32)
-    return dot(hi, same) + (dot(mid, same) + dot(low, same))
+    pieces = jnp.concatenate([hi, mid, low], axis=1)
+    return jnp.dot(pieces, same, preferred_element_type=F32)
+
+
+def each(low, high, body):
+    if isinstance(low, int) and isinstance(high, int):
+        for i in range(low, high):
+            body(i)
+    else:
+        lax.fori_loop(low, high, lambda i, _: body(i) or 0, 0)
 
 
 def work(
@@ -62,10 +70,13 @@
     msg_ref,
     sall,
     lens_ref,
+    left_ref,
+    inverse_ref,
     gsend,
     grecv,
     pgacc,
     pgrecv,
+    turned_p,
     lse_ref,
     len_ref,
     pos_ref,
@@ -129,9 +140,10 @@
         )
 
     barrier = pltpu.get_barrier_semaphore()
-    near = [
-        (d, k) for d in (3, 2, 1, -1, -2, -3, 0) for k in range(SIDES) if not (d == 0 and k == 0)
-    ]
+    near = [(d, k) for d in (0, -1, -2, -3) for k in range(SIDES) if d or k]
+    pl.semaphore_signal(
+        barrier, inc=1, device_id={"blk": b, "mp": y * CORES + other}, device_id_type=MESH
+    )
     for d, k in near:
         pl.semaphore_signal(
             barrier,
@@ -139,9 +151,13 @@
             device_id={"blk": block(d), "mp": (y + k) % SIDES * CORES + core},
             device_id_type=MESH,
         )
-    pl.semaphore_signal(
-        barrier, inc=1, device_id={"blk": b, "mp": y * CORES + other}, device_id_type=MESH
-    )
+    pl.semaphore_wait(barrier, len(near) + 1)
+
+    for i in range(WINDOW - 1):
+        s = (WINDOW - 1 - b % RING_X + i) % (WINDOW - 1) + 1
+        for k in range(SIDES):
+            send_queries(s, k).start()
+    send_queries(0, 1).start()
     get_len = pltpu.make_async_copy(len_hbm, len_ref, local.at[0])
     get_len.start()
     get_pos = pltpu.make_async_copy(pos_hbm, pos_ref, local.at[1])
@@ -150,12 +166,6 @@
     get_q.start()
     get_p = pltpu.make_async_copy(p_hbm, p_ref.at[core], local.at[3])
     get_p.start()
-    pl.semaphore_wait(barrier, len(near) + 1)
-
-    for s in (3, 2, 1, 0):
-        for k in range(SIDES):
-            if s or k:
-                send_queries(s, k).start()
     pair_p = remote(p_hbm, p_ref.at[core], pair_send.at[0], pair_recv.at[0], 0, y, other)
     pair_p.start()
 
@@ -180,17 +190,18 @@
         lax.broadcasted_iota(jnp.int32, (BLK, BLK), 0) // QTOK
         == lax.broadcasted_iota(jnp.int32, (BLK, BLK), 1) // QTOK
     ).astype(F32).astype(BF16)
-    token = (
-        lax.broadcasted_iota(jnp.int32, (TILES, 8, BLK), 0) * 4
-        + lax.broadcasted_iota(jnp.int32, (TILES, 8, BLK), 1) // 2
-    )
+    same = jnp.concatenate([same] * 3, axis=0)
+    first_token = lax.broadcasted_iota(jnp.int32, (TILES, 8, BLK), 0) * 4
     pgacc[...] = jnp.zeros_like(pgacc)
     get_p.wait()
     get_q.wait()
     pair_p.wait_recv()
     pair_len.wait_recv()
-
-    def score_block(s, _):
+    log_len = jnp.log(jnp.where(half == 0, lens_ref[0], lens_ref[1])) * QTOK
+    for h in range(CORES):
+        left_ref[h] = lens_ref[h].astype(jnp.int32) - row8 // 2
+
+    def score_block(s):
         def arrived(side):
             remote(
                 q_hbm, qall.at[s, side], q_send.at[0], q_recv.at[s * SIDES + side], 0, side, core
@@ -203,33 +214,46 @@
             arrived(y)
 
         q_blk = qall[s].reshape(BLK, DIM)
-        scores = []
+        tops = []
+        totals = []
         for h in range(CORES):
             logits = lax.dot_general(
                 p_ref[h], q_blk, (((1,), (1,)), ((), ())), preferred_element_type=F32
             ).reshape(TILES, 8, BLK)
-            lens = lens_ref[h]
-            logits = jnp.where(token < lens.astype(jnp.int32)[None], logits, NEG)
+            logits = jnp.where(left_ref[h][None] > first_token, logits, NEG)
             top = max_pairs(jnp.max(logits, axis=0))
             terms = jnp.exp2((logits - top[None]) * (ROOT * math.log2(math.e)))
+            w_ref[s, h] = terms
             total = spread_pairs(jnp.sum(terms, axis=0))
-            w_ref[s, h] = terms * (1.0 / total)[None]
-            scores.append(token_sum(top * ROOT + jnp.log(total), same) - jnp.log(lens) * QTOK)
-        message = jnp.where(half == 0, scores[0], scores[1])
+            inverse_ref[s, h] = 1.0 / total
+            tops.append(top)
+            totals.append(total)
+        top = jnp.where(half == 0, tops[0], tops[1])
+        total = jnp.where(half == 0, totals[0], totals[1])
+        message = token_sum(top * ROOT + jnp.log(total), same) - log_len
         msg_ref[s] = message
         sall[s, s * SIDES + y] = message
-        for u in range(WINDOW):
-            t = (s + 1 + u) % WINDOW
-            send_scores(s, t, 1).start()
-            if u < WINDOW - 1:
-                send_scores(s, t, 0).start()
-        return 0
-
-    def grad_block(s, _):
+        send_scores(s, s, 1).start()
+
+        def ahead(t):
+            for k in range(SIDES):
+                send_scores(s, t, k).start()
+
+        each(s + 1, WINDOW, ahead)
+
+    def behind_block(s):
+        def behind(t):
+            for k in range(SIDES):
+                send_scores(s, t, k).start()
+
+        each(0, s, behind)
+
+    def grad_block(s):
         for j in range(WINDOW):
-            for side in range(SIDES):
-
-                @pl.when((s != j) | (y != side))
+            for k in range(SIDES):
+                side = (y + k) % SIDES
+
+                @pl.when((s != j) | (k > 0))
                 def _():
                     remote(
                         msg_ref.at[0],
@@ -254,16 +278,14 @@
         coef = jnp.exp(msg_ref[s] - lse) - jnp.where(here, 1.0, 0.0)
         turned = pltpu.roll(coef, 2, 0)
         q_blk = qall[s].reshape(BLK, DIM)
-        dq = jnp.zeros((BLK, DIM), F32)
         rows = []
+        dq = jnp.zeros((DIM, BLK), F32)
         for h in range(CORES):
             c = jnp.where(half == h, coef, turned)
-            d_rows = (w_ref[s, h] * c[None]).reshape(ROWS, BLK).astype(BF16)
-            rows.append(d_rows)
-            dq = dq + lax.dot_general(
-                d_rows, p_ref[h], (((0,), (0,)), ((), ())), preferred_element_type=F32
-            )
-        gsend[s] = dq.astype(BF16).reshape(SIDES, OWN, DIM)
+            c = c * inverse_ref[s, h]
+            rows.append((w_ref[s, h] * c[None]).reshape(ROWS, BLK).astype(BF16))
+            dq = dq + jnp.dot(turned_p[h], rows[h], preferred_element_type=F32)
+        gsend[s] = dq.T.astype(BF16).reshape(SIDES, OWN, DIM)
         send_grads(s, 1).start()
 
         @pl.when(s > 0)
@@ -272,18 +294,22 @@
 
         for h in range(CORES):
             pgacc[h] += jnp.dot(rows[h], q_blk, preferred_element_type=F32)
-        return 0
-
-    early = jnp.where(b % LAYER < RING_X, b % RING_X + 1, WINDOW)
-
-    def run(g, _):
-        low = g * early
-        high = early + g * (WINDOW - early)
-        lax.fori_loop(low, high, score_block, 0)
-        lax.fori_loop(low, high, grad_block, 0)
-        return 0
-
-    lax.fori_loop(0, 2, run, 0)
+
+    def run(low, high):
+        each(low, high, score_block)
+        each(low, high, behind_block)
+        each(0, high - low, lambda i: grad_block(high - 1 - i))
+
+    place_x = b % RING_X
+    first_layer = b % LAYER < RING_X
+    early = jnp.where(first_layer, place_x + 1, WINDOW)
+    each(0, early, score_block)
+    each(0, early, behind_block)
+    for h in range(CORES):
+        turned_p[h] = p_ref[h].astype(F32).T.astype(BF16)
+    each(0, early, lambda i: grad_block(early - 1 - i))
+    for x in range(WINDOW - 1):
+        pl.when(first_layer & (place_x == x))(functools.partial(run, x + 1, WINDOW))
 
     pair_pg = remote(pgacc.at[other], pgrecv, pair_send.at[2], pair_recv.at[2], 0, y, other)
     pair_pg.start()
@@ -362,10 +388,13 @@
             pltpu.VMEM((WINDOW, 8, BLK), F32),
             pltpu.VMEM((WINDOW, slots, 8, BLK), F32),
             pltpu.VMEM((CORES, 8, BLK), F32),
+            pltpu.VMEM((CORES, 8, BLK), jnp.int32),
+            pltpu.VMEM((WINDOW, CORES, 8, BLK), F32),
             pltpu.VMEM((WINDOW, SIDES, OWN, DIM), BF16),
             pltpu.VMEM((slots, OWN, DIM), BF16),
             pltpu.VMEM((CORES, ROWS, DIM), F32),
             pltpu.VMEM((ROWS, DIM), F32),
+            pltpu.VMEM((CORES, DIM, ROWS), BF16),
             pltpu.VMEM((WINDOW, 8, BLK), F32),
             pltpu.SMEM((PER,), jnp.int32),
             pltpu.SMEM((1, WINDOW * PER), jnp.int32),
@@ -389,7 +418,7 @@
         in_specs=[vmem] * 3,
         out_specs=(hbm,) * 3,
         scratch_shapes=[dma((3,))],
-    )(*results)
+    )(*(pltpu.with_memory_space_constraint(x, pltpu.VMEM) for x in results))
     return (
         loss.reshape(PER),
         qg.reshape(PER, QTOK, DIM),

time: 41.3 us -> 31.9 us (0.77)
  Pallas kernels: 38.6 us -> 31.1 us
  local copies, waits for them, and re-layouts: 1.86 us -> 0 us
    pallas_call x1, Pallas kernels: 37 us -> 30.4 us  [on_device(): pl.pallas_call(functools.partial(work, blocks), out_shape=tuple((pltpu.VM...]
    unnamed x6 -> x0, local copies, waits for them, and re-layouts: 1.86 us -> none
    pallas_call x1, Pallas kernels: 1.65 us -> 0.71 us  [on_device(): pl.pallas_call(store, out_shape=tuple((pltpu.HBM(s, F32) for s in shapes)...]
where the time goes in v4:
time: 31.9 us; the launch traced here: 31.7 us
  Pallas kernels  31.1 us (97%)
  between operations  0.64 us (2%)
    pallas_call x1, Pallas kernels, on_device(): pl.pallas_call(functools.partial(work, blocks), out_shape=tuple((pltpu.VM...  30.4 us
    pallas_call x1, Pallas kernels, on_device(): pl.pallas_call(store, out_shape=tuple((pltpu.HBM(s, F32) for s in shapes)...  0.71 us

profile of v4, /device:TPU:1, one launch (start us, length us, event | category | flops | bytes accessed | tf_op | source)
XLA Modules:
  0.0 31.7 jit_solution(3613065871407803648)
XLA Ops:
  0.6 30.4 %shard_map.67 = (f32[1,2]{1,0:T(1,128)S(1)}, f32[64,128]{1,0:T(8,128)S(1)}, f32[360,128]{1,0:T(8,128)S(1)}) custom-call(bf16[64,128]{1,0:T(8,128)(2,1)} %bitcast.10, bf16[360,128]{1,0:T(8,128)(2,1)} %bitcast.9, s32[2]{0:T(128)} %len_hbm.1, s32[1,8]{1,0:T(1,128)} %pos_hbm.1), custom_call_target="tpu_custom_call" | custom-call | tf_op jit(solution)/shard_map/pallas_call | solution.py:379
  31.0 0.7 %shard_map.68 = (f32[1,2]{1,0:T(1,128)}, f32[64,128]{1,0:T(8,128)}, f32[360,128]{1,0:T(8,128)}) custom-call(f32[1,2]{1,0:T(1,128)S(1)} %get-tuple-element.9.loss_ref, f32[64,128]{1,0:T(8,128)S(1)} %get-tuple-element.10.qg_ref, f32[360,128]{1,0:T(8,128)S(1)} %get-tuple-element.11.pg_ref), custom_call_target="tpu_custom_call" | custom-call | tf_op jit(solution)/shard_map/pallas_call | solution.py:415

commit v5 on v4

--- a/solution.py
+++ b/solution.py
@@ -12,6 +12,7 @@
 SIDES = 2
 CORES = 2
 PER = 2
+CANDS = CORES * PER
 QTOK = 32
 PTOK = 180
 DIM = 128
@@ -67,6 +68,7 @@
     qall,
     p_ref,
     w_ref,
+    own_ref,
     msg_ref,
     sall,
     lens_ref,
@@ -119,7 +121,7 @@
         side = (y + k) % SIDES
         return remote(
             msg_ref.at[s],
-            sall.at[t, s * SIDES + y],
+            sall.at[t, s, y],
             s_send.at[(s * WINDOW + t) * SIDES + k],
             s_recv.at[(t * WINDOW + s) * SIDES + y],
             t - s,
@@ -231,8 +233,9 @@
         top = jnp.where(half == 0, tops[0], tops[1])
         total = jnp.where(half == 0, totals[0], totals[1])
         message = token_sum(top * ROOT + jnp.log(total), same) - log_len
-        msg_ref[s] = message
-        sall[s, s * SIDES + y] = message
+        own_ref[s] = message
+        msg_ref[s] = message[:CANDS]
+        sall[s, s, y] = message[:CANDS]
         send_scores(s, s, 1).start()
 
         def ahead(t):
@@ -257,7 +260,7 @@
                 def _():
                     remote(
                         msg_ref.at[0],
-                        sall.at[s, j * SIDES + side],
+                        sall.at[s, j, side],
                         s_send.at[0],
                         s_recv.at[(s * WINDOW + j) * SIDES + side],
                         0,
@@ -266,16 +269,13 @@
                     ).wait_recv()
 
         tile = sall[s]
-        top = jnp.max(tile, axis=0)
-        top = jnp.maximum(top, pltpu.roll(top, 1, 0))
-        top = jnp.maximum(top, pltpu.roll(top, 2, 0))
-        total = jnp.sum(jnp.exp(tile - top[None]), axis=0)
-        total = total + pltpu.roll(total, 1, 0)
-        total = total + pltpu.roll(total, 2, 0)
-        lse = top + jnp.log(total)
+        top = jnp.max(jnp.max(tile, axis=(0, 1)), axis=0, keepdims=True)
+        terms = jnp.sum(jnp.exp(tile - top[None, None]), axis=(0, 1))
+        lse = top + jnp.log(jnp.sum(terms, axis=0, keepdims=True))
+        lse = jnp.broadcast_to(lse, (8, BLK))
         lse_ref[s] = lse
         here = (pos == y * (CORES * PER) + row8 % (CORES * PER)) & (s == 0)
-        coef = jnp.exp(msg_ref[s] - lse) - jnp.where(here, 1.0, 0.0)
+        coef = jnp.exp(own_ref[s] - lse) - jnp.where(here, 1.0, 0.0)
         turned = pltpu.roll(coef, 2, 0)
         q_blk = qall[s].reshape(BLK, DIM)
         rows = []
@@ -314,10 +314,10 @@
     pair_pg = remote(pgacc.at[other], pgrecv, pair_send.at[2], pair_recv.at[2], 0, y, other)
     pair_pg.start()
 
-    found = jnp.zeros((8, BLK), F32)
+    found = jnp.zeros((CANDS, BLK), F32)
     for side in range(SIDES):
-        here = (pos == side * (CORES * PER) + row8) & (row8 < CORES * PER)
-        found = found + jnp.where(here, sall[0, side], 0.0)
+        here = pos[:CANDS] == side * CANDS + row8[:CANDS]
+        found = found + jnp.where(here, sall[0, 0, side], 0.0)
     loss = lse_ref[0][0:1] - jnp.sum(found, axis=0, keepdims=True)
     one = [
         jnp.sum(jnp.where(lane8[0:1] == y * OWN + n * QTOK, loss, 0.0)) for n in range(PER)
@@ -386,7 +386,8 @@
             pltpu.VMEM((CORES, ROWS, DIM), BF16),
             pltpu.VMEM((WINDOW, CORES, TILES, 8, BLK), F32),
             pltpu.VMEM((WINDOW, 8, BLK), F32),
-            pltpu.VMEM((WINDOW, slots, 8, BLK), F32),
+            pltpu.VMEM((WINDOW, CANDS, BLK), F32),
+            pltpu.VMEM((WINDOW, WINDOW, SIDES, CANDS, BLK), F32),
             pltpu.VMEM((CORES, 8, BLK), F32),
             pltpu.VMEM((CORES, 8, BLK), jnp.int32),
             pltpu.VMEM((WINDOW, CORES, 8, BLK), F32),

time: 31.9 us -> 31.2 us (0.978)
  Pallas kernels: 31.1 us -> 30.4 us
    pallas_call x1, Pallas kernels: 30.4 us -> 29.7 us  [on_device(): pl.pallas_call(functools.partial(work, blocks), out_shape=tuple((pltpu.VM...]
where the time goes in v5:
time: 31.2 us; the launch traced here: 31 us
  Pallas kernels  30.4 us (97%)
  between operations  0.64 us (2%)
    pallas_call x1, Pallas kernels, on_device(): pl.pallas_call(functools.partial(work, blocks), out_shape=tuple((pltpu.VM...  29.7 us
    pallas_call x1, Pallas kernels, on_device(): pl.pallas_call(store, out_shape=tuple((pltpu.HBM(s, F32) for s in shapes)...  0.71 us

profile of v5, /device:TPU:1, one launch (start us, length us, event | category | flops | bytes accessed | tf_op | source)
XLA Modules:
  0.0 31.0 jit_solution(6419905566315680456)
XLA Ops:
  0.6 29.7 %shard_map.67 = (f32[1,2]{1,0:T(1,128)S(1)}, f32[64,128]{1,0:T(8,128)S(1)}, f32[360,128]{1,0:T(8,128)S(1)}) custom-call(bf16[64,128]{1,0:T(8,128)(2,1)} %bitcast.10, bf16[360,128]{1,0:T(8,128)(2,1)} %bitcast.9, s32[2]{0:T(128)} %len_hbm.1, s32[1,8]{1,0:T(1,128)} %pos_hbm.1), custom_call_target="tpu_custom_call" | custom-call | tf_op jit(solution)/shard_map/pallas_call | solution.py:379
  30.3 0.7 %shard_map.68 = (f32[1,2]{1,0:T(1,128)}, f32[64,128]{1,0:T(8,128)}, f32[360,128]{1,0:T(8,128)}) custom-call(f32[1,2]{1,0:T(1,128)S(1)} %get-tuple-element.9.loss_ref, f32[64,128]{1,0:T(8,128)S(1)} %get-tuple-element.10.qg_ref, f32[360,128]{1,0:T(8,128)S(1)} %get-tuple-element.11.pg_ref), custom_call_target="tpu_custom_call" | custom-call | tf_op jit(solution)/shard_map/pallas_call | solution.py:416

commit v6 on v5

--- a/solution.py
+++ b/solution.py
@@ -114,7 +114,7 @@
     def send_queries(s, k):
         side = (y + k) % SIDES
         return remote(
-            q_hbm, qall.at[s, y], q_send.at[s * SIDES + k], q_recv.at[s * SIDES + y], s, side, core
+            qall.at[0, y], qall.at[s, y], q_send.at[s * SIDES + k], q_recv.at[s * SIDES + y], s, side, core
         )
 
     def send_scores(s, t, k):
@@ -142,24 +142,9 @@
         )
 
     barrier = pltpu.get_barrier_semaphore()
-    near = [(d, k) for d in (0, -1, -2, -3) for k in range(SIDES) if d or k]
     pl.semaphore_signal(
         barrier, inc=1, device_id={"blk": b, "mp": y * CORES + other}, device_id_type=MESH
     )
-    for d, k in near:
-        pl.semaphore_signal(
-            barrier,
-            inc=1,
-            device_id={"blk": block(d), "mp": (y + k) % SIDES * CORES + core},
-            device_id_type=MESH,
-        )
-    pl.semaphore_wait(barrier, len(near) + 1)
-
-    for i in range(WINDOW - 1):
-        s = (WINDOW - 1 - b % RING_X + i) % (WINDOW - 1) + 1
-        for k in range(SIDES):
-            send_queries(s, k).start()
-    send_queries(0, 1).start()
     get_len = pltpu.make_async_copy(len_hbm, len_ref, local.at[0])
     get_len.start()
     get_pos = pltpu.make_async_copy(pos_hbm, pos_ref, local.at[1])
@@ -168,7 +153,25 @@
     get_q.start()
     get_p = pltpu.make_async_copy(p_hbm, p_ref.at[core], local.at[3])
     get_p.start()
-    pair_p = remote(p_hbm, p_ref.at[core], pair_send.at[0], pair_recv.at[0], 0, y, other)
+
+    near = [(d, k) for d in (0, -1, -2, -3) for k in range(SIDES) if d or k]
+    for d, k in near:
+        pl.semaphore_signal(
+            barrier,
+            inc=1,
+            device_id={"blk": block(d), "mp": (y + k) % SIDES * CORES + core},
+            device_id_type=MESH,
+        )
+    get_q.wait()
+    pl.semaphore_wait(barrier, len(near) + 1)
+
+    for i in range(WINDOW - 1):
+        s = (WINDOW - 1 - b % RING_X + i) % (WINDOW - 1) + 1
+        for k in range(SIDES):
+            send_queries(s, k).start()
+    send_queries(0, 1).start()
+    get_p.wait()
+    pair_p = remote(p_ref.at[core], p_ref.at[core], pair_send.at[0], pair_recv.at[0], 0, y, other)
     pair_p.start()
 
     row8 = lax.broadcasted_iota(jnp.int32, (8, BLK), 0)
@@ -195,8 +198,6 @@
     same = jnp.concatenate([same] * 3, axis=0)
     first_token = lax.broadcasted_iota(jnp.int32, (TILES, 8, BLK), 0) * 4
     pgacc[...] = jnp.zeros_like(pgacc)
-    get_p.wait()
-    get_q.wait()
     pair_p.wait_recv()
     pair_len.wait_recv()
     log_len = jnp.log(jnp.where(half == 0, lens_ref[0], lens_ref[1])) * QTOK
@@ -335,20 +336,23 @@
                 ).wait_recv()
                 qg = qg + grecv[i].astype(F32)
     qg_ref[...] = qg * ROOT
+    for s in range(WINDOW):
+        for k in range(SIDES):
+            if s or k:
+                send_queries(s, k).wait_send()
+            for t in range(WINDOW):
+                if s != t or k:
+                    send_scores(s, t, k).wait_send()
+    pair_p.wait_send()
+    pair_len.wait_send()
     pair_pg.wait_recv()
     pg_ref[...] = (pgacc[core] + pgrecv[...]) * ROOT
 
-    pair_p.wait_send()
-    pair_len.wait_send()
     pair_pg.wait_send()
     for s in range(WINDOW):
         for k in range(SIDES):
             if s or k:
-                send_queries(s, k).wait_send()
                 send_grads(s, k).wait_send()
-            for t in range(WINDOW):
-                if s != t or k:
-                    send_scores(s, t, k).wait_send()
 
 
 def store(loss_ref, qg_ref, pg_ref, loss_out, qg_out, pg_out, sems):

time: 31.2 us -> 31 us (level)
  no operation moved by 1% of the time
where the time goes in v6:
time: 31 us; the launch traced here: 30.8 us
  Pallas kernels  30.2 us (97%)
  between operations  0.64 us (2%)
    pallas_call x1, Pallas kernels, on_device(): pl.pallas_call(functools.partial(work, blocks), out_shape=tuple((pltpu.VM...  29.5 us
    pallas_call x1, Pallas kernels, on_device(): pl.pallas_call(store, out_shape=tuple((pltpu.HBM(s, F32) for s in shapes)...  0.71 us

profile of v6, /device:TPU:1, one launch (start us, length us, event | category | flops | bytes accessed | tf_op | source)
XLA Modules:
  0.0 30.8 jit_solution(11731680188064171822)
XLA Ops:
  0.6 29.5 %shard_map.67 = (f32[1,2]{1,0:T(1,128)S(1)}, f32[64,128]{1,0:T(8,128)S(1)}, f32[360,128]{1,0:T(8,128)S(1)}) custom-call(bf16[64,128]{1,0:T(8,128)(2,1)} %bitcast.10, bf16[360,128]{1,0:T(8,128)(2,1)} %bitcast.9, s32[2]{0:T(128)} %len_hbm.1, s32[1,8]{1,0:T(1,128)} %pos_hbm.1), custom_call_target="tpu_custom_call" | custom-call | tf_op jit(solution)/shard_map/pallas_call | solution.py:383
  30.1 0.7 %shard_map.68 = (f32[1,2]{1,0:T(1,128)}, f32[64,128]{1,0:T(8,128)}, f32[360,128]{1,0:T(8,128)}) custom-call(f32[1,2]{1,0:T(1,128)S(1)} %get-tuple-element.9.loss_ref, f32[64,128]{1,0:T(8,128)S(1)} %get-tuple-element.10.qg_ref, f32[360,128]{1,0:T(8,128)S(1)} %get-tuple-element.11.pg_ref), custom_call_target="tpu_custom_call" | custom-call | tf_op jit(solution)/shard_map/pallas_call | solution.py:420

commit v7 on v6

--- a/solution.py
+++ b/solution.py
@@ -77,6 +77,7 @@
     gsend,
     grecv,
     pgacc,
+    pgsend,
     pgrecv,
     turned_p,
     lse_ref,
@@ -162,6 +163,7 @@
             device_id={"blk": block(d), "mp": (y + k) % SIDES * CORES + core},
             device_id_type=MESH,
         )
+    pgacc[...] = jnp.zeros_like(pgacc)
     get_q.wait()
     pl.semaphore_wait(barrier, len(near) + 1)
 
@@ -197,7 +199,6 @@
     ).astype(F32).astype(BF16)
     same = jnp.concatenate([same] * 3, axis=0)
     first_token = lax.broadcasted_iota(jnp.int32, (TILES, 8, BLK), 0) * 4
-    pgacc[...] = jnp.zeros_like(pgacc)
     pair_p.wait_recv()
     pair_len.wait_recv()
     log_len = jnp.log(jnp.where(half == 0, lens_ref[0], lens_ref[1])) * QTOK
@@ -312,7 +313,8 @@
     for x in range(WINDOW - 1):
         pl.when(first_layer & (place_x == x))(functools.partial(run, x + 1, WINDOW))
 
-    pair_pg = remote(pgacc.at[other], pgrecv, pair_send.at[2], pair_recv.at[2], 0, y, other)
+    pgsend[...] = pgacc[other].astype(BF16)
+    pair_pg = remote(pgsend, pgrecv, pair_send.at[2], pair_recv.at[2], 0, y, other)
     pair_pg.start()
 
     found = jnp.zeros((CANDS, BLK), F32)
@@ -346,7 +348,7 @@
     pair_p.wait_send()
     pair_len.wait_send()
     pair_pg.wait_recv()
-    pg_ref[...] = (pgacc[core] + pgrecv[...]) * ROOT
+    pg_ref[...] = (pgacc[core] + pgrecv[...].astype(F32)) * ROOT
 
     pair_pg.wait_send()
     for s in range(WINDOW):
@@ -398,7 +400,8 @@
             pltpu.VMEM((WINDOW, SIDES, OWN, DIM), BF16),
             pltpu.VMEM((slots, OWN, DIM), BF16),
             pltpu.VMEM((CORES, ROWS, DIM), F32),
-            pltpu.VMEM((ROWS, DIM), F32),
+            pltpu.VMEM((ROWS, DIM), BF16),
+            pltpu.VMEM((ROWS, DIM), BF16),
             pltpu.VMEM((CORES, DIM, ROWS), BF16),
             pltpu.VMEM((WINDOW, 8, BLK), F32),
             pltpu.SMEM((PER,), jnp.int32),

time: 31 us -> 30.8 us (level)
  no operation moved by 1% of the time
where the time goes in v7:
time: 30.8 us; the launch traced here: 30.7 us
  Pallas kernels  30.1 us (98%)
  between operations  0.64 us (2%)
    pallas_call x1, Pallas kernels, on_device(): pl.pallas_call(functools.partial(work, blocks), out_shape=tuple((pltpu.VM...  29.4 us
    pallas_call x1, Pallas kernels, on_device(): pl.pallas_call(store, out_shape=tuple((pltpu.HBM(s, F32) for s in shapes)...  0.71 us

profile of v7, /device:TPU:1, one launch (start us, length us, event | category | flops | bytes accessed | tf_op | source)
XLA Modules:
  0.0 30.7 jit_solution(3802492855764865237)
XLA Ops:
  0.6 29.4 %shard_map.67 = (f32[1,2]{1,0:T(1,128)S(1)}, f32[64,128]{1,0:T(8,128)S(1)}, f32[360,128]{1,0:T(8,128)S(1)}) custom-call(bf16[64,128]{1,0:T(8,128)(2,1)} %bitcast.10, bf16[360,128]{1,0:T(8,128)(2,1)} %bitcast.9, s32[2]{0:T(128)} %len_hbm.1, s32[1,8]{1,0:T(1,128)} %pos_hbm.1), custom_call_target="tpu_custom_call" | custom-call | tf_op jit(solution)/shard_map/pallas_call | solution.py:385
  30.0 0.7 %shard_map.68 = (f32[1,2]{1,0:T(1,128)}, f32[64,128]{1,0:T(8,128)}, f32[360,128]{1,0:T(8,128)}) custom-call(f32[1,2]{1,0:T(1,128)S(1)} %get-tuple-element.9.loss_ref, f32[64,128]{1,0:T(8,128)S(1)} %get-tuple-element.10.qg_ref, f32[360,128]{1,0:T(8,128)S(1)} %get-tuple-element.11.pg_ref), custom_call_target="tpu_custom_call" | custom-call | tf_op jit(solution)/shard_map/pallas_call | solution.py:423
